TPU v7x, 256 devices: a whole 4x4x8 slice. The times are simulated.
256 devices in a mesh: dp: 16 (over x, y), ctx: 16 (over z, core).
Axes of the slice: x: 4, y: 4, z: 8, core: 2. Of those that a mesh axis runs over, the one named last changes fastest.
Arguments:
- frames: bfloat16 [512, 256, 1408], P(('dp', 'ctx')), may hold values from -6 to 6
- cotangent: bfloat16 [512, 256, 1408], P(('dp', 'ctx')), may hold values from -6 to 6
- clip_ids: int32 [16, 32], P('dp'), may hold values from 0 to 2, never falling along the last dimension, each value on 1 to 24 neighbouring positions
- gain: float32 [1408], replicated, may hold values from 0.1 to 1.9
- query_key_value_weight: bfloat16 [1408, 2112], replicated, may hold values from -4 to 4
- w_out: bfloat16 [704, 1408], replicated, may hold values from -0.21875 to 0.21875
Outputs:
- frame_input_gradient: bfloat16 [512, 256, 1408], P(('dp', 'ctx'))
- gain_grad: float32 [1408], replicated
Inputs may be any that keep to these rules, and one draw needn't show every extreme that they name: `clip_ids`: in each row (one group of 32 frames) ids never fall; each of the 3 clips holds 1 to 24 consecutive frames and one holds exactly 24.
All inputs are finite; a program needn't handle non-finite values.
Results may differ from a plain program's by a relative error of at most 0.005.
The roundings to bfloat16 on the way count: a program that leaves them out, or rounds other values in their place, can miss the bound.
Values may be sent and summed in bfloat16 or wider, within the bound.
No kernel may reach another device: no remote copies, remote signals or barrier semaphores. Data moves between devices by JAX's collectives and lax.ppermute only.
A program may use at most 64 MiB of HBM per device.

v0:
```python
import math

import jax
import jax.numpy as jnp
from jax import lax
from jax.sharding import PartitionSpec as P

HEADS = 8


def apply_norm(frames, gain):
    values = frames.astype(jnp.float32)
    centered_values = values - jnp.mean(values, axis=-1, keepdims=True)
    inverse_deviation = lax.rsqrt(
        jnp.mean(centered_values * centered_values, axis=-1, keepdims=True) + 1e-05
    )
    standardized_input = centered_values * inverse_deviation
    return ((standardized_input * gain).astype(jnp.bfloat16), standardized_input, inverse_deviation)


def norm_backward(normed_gradient, standardized_input, inverse_deviation, gain):
    expanded_values = normed_gradient * gain
    first_term = jnp.mean(expanded_values, axis=-1, keepdims=True)
    second_term = jnp.mean(expanded_values * standardized_input, axis=-1, keepdims=True)
    return inverse_deviation * (expanded_values - first_term - standardized_input * second_term)


def split_heads(block, heads):
    return block.reshape(block.shape[0], block.shape[1], heads, -1)


def attend(query_key_value, same, heads):
    inner = query_key_value.shape[-1] // 3
    query = split_heads(query_key_value[..., :inner], heads)
    keys = split_heads(query_key_value[..., inner : 2 * inner], heads)
    scale = 1.0 / math.sqrt(inner // heads)
    scores = jnp.einsum("fphd,gphd->phfg", query, keys, preferred_element_type=jnp.float32) * scale
    scores = jnp.where(same, scores, -1e30)
    top = jnp.max(scores, axis=-1, keepdims=True)
    expo = jnp.exp(scores - top)
    probs = expo / jnp.sum(expo, axis=-1, keepdims=True)
    weights = probs.astype(jnp.bfloat16)
    return (probs, weights)


def attend_back(query_key_value, probs, weights, d_attn, heads):
    inner = query_key_value.shape[-1] // 3
    query = split_heads(query_key_value[..., :inner], heads)
    keys = split_heads(query_key_value[..., inner : 2 * inner], heads)
    value = split_heads(query_key_value[..., 2 * inner :], heads)
    scale = 1.0 / math.sqrt(inner // heads)
    d_heads = split_heads(d_attn, heads)
    d_weights = jnp.einsum("fphd,gphd->phfg", d_heads, value, preferred_element_type=jnp.float32)
    d_value = jnp.einsum("phfg,fphd->gphd", weights, d_heads, preferred_element_type=jnp.float32)
    d_scores = probs * (d_weights - jnp.sum(probs * d_weights, axis=-1, keepdims=True))
    d_scores = d_scores.astype(jnp.bfloat16)
    d_query = (
        jnp.einsum("phfg,gphd->fphd", d_scores, keys, preferred_element_type=jnp.float32) * scale
    )
    d_key = (
        jnp.einsum("phfg,fphd->gphd", d_scores, query, preferred_element_type=jnp.float32) * scale
    )
    lead = (query_key_value.shape[0], query_key_value.shape[1], inner)
    joined = jnp.concatenate(
        [d_query.reshape(lead), d_key.reshape(lead), d_value.reshape(lead)], axis=-1
    )
    return joined.astype(jnp.bfloat16)


def input_projection(frames, gain, query_key_value_weight):
    normalized_frames, standardized_input, inverse_deviation = apply_norm(frames, gain)
    query_key_value = jnp.dot(
        normalized_frames.reshape(-1, frames.shape[2]),
        query_key_value_weight,
        preferred_element_type=jnp.float32,
    )
    query_key_value = query_key_value.astype(jnp.bfloat16).reshape(
        frames.shape[:2] + (query_key_value_weight.shape[1],)
    )
    return (standardized_input, inverse_deviation, query_key_value)


def cot_in(cotangent, w_out):
    flat = cotangent.reshape(-1, cotangent.shape[2])
    d_attn = lax.dot_general(
        flat, w_out, (((1,), (1,)), ((), ())), preferred_element_type=jnp.float32
    )
    return d_attn.astype(jnp.bfloat16).reshape(cotangent.shape[:2] + (w_out.shape[0],))


def final_result(
    frames,
    cotangent,
    standardized_input,
    inverse_deviation,
    gain,
    query_key_value_gradient,
    query_key_value_weight,
):
    flat = query_key_value_gradient.reshape(-1, query_key_value_gradient.shape[2])
    normed_gradient = lax.dot_general(
        flat, query_key_value_weight, (((1,), (1,)), ((), ())), preferred_element_type=jnp.float32
    )
    normed_gradient = normed_gradient.reshape(frames.shape)
    frame_input_gradient = (
        cotangent.astype(jnp.float32)
        + norm_backward(normed_gradient, standardized_input, inverse_deviation, gain)
    ).astype(jnp.bfloat16)
    partial_term = jnp.sum(
        (normed_gradient * standardized_input).reshape(-1, frames.shape[2]), axis=0
    )
    return (frame_input_gradient, partial_term)


def on_device(frames, cotangent, clip_ids, gain, query_key_value_weight, w_out):
    clip_row = clip_ids[0]
    same = clip_row[:, None] == clip_row[None, :]
    groups = lax.axis_size("dp")
    members = lax.axis_size("ctx")
    count = groups * members * frames.shape[0] * frames.shape[1]
    standardized_input, inverse_deviation, query_key_value = input_projection(
        frames, gain, query_key_value_weight
    )
    qkv_moved = lax.all_to_all(query_key_value, "ctx", split_axis=1, concat_axis=0, tiled=True)
    probs, weights = attend(qkv_moved, same, HEADS)
    d_attn = cot_in(cotangent, w_out)
    d_attn_moved = lax.all_to_all(d_attn, "ctx", split_axis=1, concat_axis=0, tiled=True)
    dqkv_moved = attend_back(qkv_moved, probs, weights, d_attn_moved, HEADS)
    query_key_value_gradient = lax.all_to_all(
        dqkv_moved, "ctx", split_axis=0, concat_axis=1, tiled=True
    )
    frame_input_gradient, partial_term = final_result(
        frames,
        cotangent,
        standardized_input,
        inverse_deviation,
        gain,
        query_key_value_gradient,
        query_key_value_weight,
    )
    total = lax.psum(partial_term, ("dp", "ctx"))
    return (frame_input_gradient, total * (1.0 / math.sqrt(count)))


def solution(mesh):
    return jax.shard_map(
        on_device,
        mesh=mesh,
        in_specs=(
            P(("dp", "ctx"), None, None),
            P(("dp", "ctx"), None, None),
            P("dp", None),
            P(),
            P(),
            P(),
        ),
        out_specs=(P(("dp", "ctx"), None, None), P()),
        check_vma=False,
    )
```

profile of v0, /device:TPU:1, one launch (start us, length us, event | category | flops | bytes accessed | tf_op | source)
XLA Modules:
  0.0 300.8 jit_solution(3744791833389872013)
XLA Ops:
  0.6 0.0 copy-start
  0.6 1.5 copy-done
  2.2 3.5 %convolution_convert_fusion.2 = bf16[512,704]{0,1:T(8,128)(2,1)} fusion(bf16[512,1408]{1,0:T(8,128)(2,1)} %bitcast.49, bf16[704,1408]{1,0:T(8,128)(2,1)S(1)} %copy-done), kind=kOutput, calls=%fused_computation.29 | convolution fusion | flops 1015382016 | bytes 4145152 | tf_op jit(solution)/shard_map/dot_general | solution.py:85
  5.7 0.0 copy-start.1
  5.7 2.9 reshape.79
  8.6 3.6 %copy.31 = bf16[2,256,704]{2,0,1:T(2,128)(2,1)} copy(bf16[2,256,704]{1,0,2:T(2,128)(2,1)} %reshape.79) | data formatting | bytes 1441792 | tf_op jit(solution)/shard_map/reshape | solution.py:88
  12.2 0.0 copy-start.6
  12.2 10.1 %all-to-all-start.1 = ((bf16[2,256,704]{2,0,1:T(2,128)(2,1)}), bf16[2,256,704]{2,0,1:T(2,128)(2,1)}, u32[]{:S(2)}, u32[]{:S(2)}) async-start(bf16[2,256,704]{2,0,1:T(2,128)(2,1)} %copy.31), calls=%async_computation.1 | async-start | bytes 1572864 | tf_op jit(solution)/shard_map/all_to_all | solution.py:127
  22.4 0.0 copy-done.1
  22.4 0.3 convert_reduce_fusion
  22.6 0.5 fusion.16
  23.2 0.0 copy-done.6
  23.2 0.5 fusion.9
  23.7 7.5 %convolution_convert_fusion = bf16[512,2112]{0,1:T(8,128)(2,1)} fusion(bf16[512,1408]{1,0:T(8,128)(2,1)S(1)} %bitcast.50, bf16[1408,2112]{0,1:T(8,128)(2,1)} %param.10), kind=kOutput, calls=%fused_computation.3 | convolution fusion | flops 3046146048 | bytes 9551872 | tf_op jit(solution)/shard_map/dot_general | solution.py:72
  31.2 5.4 %reshape.75 = bf16[2,256,2112]{1,0,2:T(2,128)(2,1)} reshape(bf16[512,2112]{0,1:T(8,128)(2,1)} %convolution_convert_fusion) | data formatting | bytes 4325376 | tf_op jit(solution)/shard_map/reshape | solution.py:77
  36.6 8.6 %copy.26 = bf16[2,256,2112]{2,0,1:T(2,128)(2,1)} copy(bf16[2,256,2112]{1,0,2:T(2,128)(2,1)} %reshape.75) | data formatting | bytes 4325376 | tf_op jit(solution)/shard_map/reshape | solution.py:77
  45.2 0.0 copy-start.7
  45.2 0.0 all-to-all-done.1
  45.2 7.4 %all-to-all-start = ((bf16[2,256,2112]{2,0,1:T(2,128)(2,1)}), bf16[2,256,2112]{2,0,1:T(2,128)(2,1)}, u32[]{:S(2)}, u32[]{:S(2)}) async-start(bf16[2,256,2112]{2,0,1:T(2,128)(2,1)} %copy.26), calls=%async_computation | async-start | bytes 4456448 | tf_op jit(solution)/shard_map/all_to_all | solution.py:124
  52.6 0.0 copy-done.7
  52.6 0.1 broadcast_compare_fusion
  52.7 1.2 copy.32
  53.9 1.0 copy.33
  54.9 3.1 %reshape.80 = bf16[32,16,8,88]{3,2,1,0:T(8,128)(2,1)} reshape(bf16[16,2,16,704]{3,2,1,0:T(8,128)(2,1)} %copy.33) | data formatting | bytes 1441792 | tf_op jit(solution)/shard_map/reshape | solution.py:29
  57.9 46.4 %all-to-all-done = bf16[2,256,2112]{2,0,1:T(2,128)(2,1)} async-done(((bf16[2,256,2112]{2,0,1:T(2,128)(2,1)}), bf16[2,256,2112]{2,0,1:T(2,128)(2,1)}, u32[]{:S(2)}, u32[]{:S(2)}) %all-to-all-start) | async-done | bytes 2162720 | tf_op jit(solution)/shard_map/all_to_all | solution.py:124
  104.4 1.9 copy.27
  106.2 0.2 copy.28
  106.4 1.9 fusion.48
  108.2 3.1 %reshape.76 = bf16[32,16,8,88]{3,2,1,0:T(8,128)(2,1)} reshape(bf16[32,16,704]{2,1,0:T(8,128)(2,1)} %get-tuple-element.7) | data formatting | bytes 1441792 | tf_op jit(solution)/shard_map/reshape | solution.py:29
  111.3 3.1 %reshape.77 = bf16[32,16,8,88]{3,2,1,0:T(8,128)(2,1)} reshape(bf16[32,16,704]{2,1,0:T(8,128)(2,1)} %get-tuple-element.5) | data formatting | bytes 1441792 | tf_op jit(solution)/shard_map/reshape | solution.py:29
  114.4 3.1 %reshape.81 = bf16[32,16,8,88]{3,2,1,0:T(8,128)(2,1)} reshape(bf16[32,16,704]{2,1,0:T(8,128)(2,1)} %get-tuple-element.6) | data formatting | bytes 1441792 | tf_op jit(solution)/shard_map/reshape | solution.py:29
  117.5 4.8 %fusion.49 = (f32[16,8,32]{2,1,0:T(8,128)S(1)}, f32[16,8,32,32]{2,3,1,0:T(8,128)}) fusion(pred[32,32]{0,1:T(8,128)(4,1)S(1)} %broadcast_compare_fusion, bf16[32,16,8,88]{3,2,1,0:T(8,128)(2,1)} %reshape.76, bf16[32,16,8,88]{3,2,1,0:T(8,128)(2,1)} %reshape.77), kind=kOutput, calls=%fused_computation.56 | convolution fusion | flops 23592992 | bytes 1983488 | tf_op jit(solution)/shard_map/sub | solution.py:40
  122.3 0.0 copy-start.4
  122.3 4.1 %multiply_reduce_fusion.1 = (f32[16,8,32]{2,1,0:T(8,128)S(1)}, f32[16,8,32,32]{2,3,1,0:T(8,128)S(1)}) fusion(f32[16,8,32,32]{2,3,1,0:T(8,128)} %get-tuple-element.9, f32[16,8,32]{2,1,0:T(8,128)S(1)} %get-tuple-element.8, bf16[32,16,8,88]{3,2,1,0:T(8,128)(2,1)} %reshape.81, bf16[32,16,8,88]{3,2,1,0:T(8,128)(2,1)} %reshape.80), kind=kOutput, calls=%fused_computation.24 | convolution fusion | flops 23457792 | bytes 2523136 | tf_op jit(solution)/shard_map/fphd,gphd->phfg/dot_general | solution.py:53
  126.4 0.0 copy-done.4
  126.4 0.0 copy-start.3
  126.4 0.7 multiply_convert_fusion.2
  127.1 0.5 copy-done.3
  127.6 0.0 copy-start.2
  127.6 0.9 fusion.20
  128.5 0.4 copy-done.2
  128.8 0.0 copy-start.5
  128.8 1.9 fusion.19
  130.8 0.0 copy-done.5
  130.8 1.8 fusion.18
  132.6 1.4 copy.40
  134.0 2.7 reshape.83
  136.7 2.7 copy.38
  139.4 2.7 reshape.82
  142.1 2.6 copy.42
  144.7 2.7 reshape.84
  147.4 5.0 %concatenate.4 = bf16[32,16,2112]{2,1,0:T(8,128)(2,1)} concatenate(bf16[32,16,704]{2,1,0:T(8,128)(2,1)} %reshape.82, bf16[32,16,704]{2,1,0:T(8,128)(2,1)} %reshape.83, bf16[32,16,704]{2,1,0:T(8,128)(2,1)} %reshape.84), dimensions={2} | concatenate | bytes 4325376 | tf_op jit(solution)/shard_map/concatenate | solution.py:64
  152.4 59.0 %all_to_all.48 = bf16[32,16,2112]{2,1,0:T(8,128)(2,1)S(1)} all-to-all(bf16[32,16,2112]{2,1,0:T(8,128)(2,1)} %concatenate.4), channel_id=1, replica_groups=mesh['dp'=16,'ctx'=16] {'ctx'}, dimensions={0} | all-to-all | bytes 4325376 | tf_op jit(solution)/shard_map/all_to_all | solution.py:129
  211.4 0.2 copy.43
  211.5 8.3 %fusion.15 = (f32[1408]{0:T(1024)S(1)}, f32[2,256]{1,0:T(2,128)S(1)}, f32[2,256]{1,0:T(2,128)S(1)}, f32[2,256,1408]{2,1,0:T(8,128)}) fusion(bf16[2,256,1408]{2,1,0:T(8,128)(2,1)S(1)} %copy-done.1, f32[2,256]{1,0:T(2,128)S(1)} %add_rsqrt_fusion, f32[2,256]{1,0:T(2,128)S(1)} %broadcast_multiply_fusion.3, f32[1408]{0:T(1024)S(1)} %copy-done.6, ...), kind=kOutput, calls=%fused_computation.18 | convolution fusion | flops 3051550208 | bytes 12454912 | tf_op jit(solution)/shard_map/dot_general | solution.py:101
  219.8 75.9 %psum.7 = f32[1408]{0:T(1024)S(1)} all-reduce(f32[1408]{0:T(1024)S(1)} %get-tuple-element.2), channel_id=1, replica_groups=mesh['dp'=16,'ctx'=16] {'dp','ctx'}, use_global_device_ids=true, to_apply=%region_8.9 | all-reduce | flops 1408 | bytes 11264 | tf_op jit(solution)/shard_map/psum | solution.py:141
  295.7 0.6 broadcast_multiply_fusion
  296.3 4.5 %fusion.14 = bf16[2,256,1408]{2,1,0:T(8,128)(2,1)} fusion(bf16[2,256,1408]{2,1,0:T(8,128)(2,1)S(1)} %copy-done.1, bf16[2,256,1408]{2,1,0:T(8,128)(2,1)} %param.7, f32[2,256,1408]{2,1,0:T(8,128)} %get-tuple-element.12, f32[2,256]{1,0:T(2,128)S(1)} %get-tuple-element.13, f32[2,256]{1,0:T(2,128)S(1)} %get-tuple-element.14, f32[1408]{0:T(1024)S(1)} %copy-done.6, ...), kind=kLoop, calls=%fused_computation.17 | loop fusion | flops 7929856 | bytes 7222784 | tf_op jit(solution)/shard_map/convert_element_type | solution.py:108
  (3 shorter events, 0.0 us)
Async XLA Ops:
  0.6 1.6 copy-start
  5.7 16.6 %copy-start.1 = (bf16[2,256,1408]{2,1,0:T(8,128)(2,1)S(1)}, bf16[2,256,1408]{2,1,0:T(8,128)(2,1)}, u32[]{:S(2)}) copy-start(bf16[2,256,1408]{2,1,0:T(8,128)(2,1)} %param.6) | copy-start | bytes 4325380
  12.2 10.9 %copy-start.6 = (f32[1408]{0:T(1024)S(1)}, f32[1408]{0:T(1024)}, u32[]{:S(2)}) copy-start(f32[1408]{0:T(1024)} %param.9) | copy-start | bytes 16900
  12.2 33.0 %all-to-all-start.1 = ((bf16[2,256,704]{2,0,1:T(2,128)(2,1)}), bf16[2,256,704]{2,0,1:T(2,128)(2,1)}, u32[]{:S(2)}, u32[]{:S(2)}) async-start(bf16[2,256,704]{2,0,1:T(2,128)(2,1)} %copy.31), calls=%async_computation.1 | async-start | bytes 1572864 | tf_op jit(solution)/shard_map/all_to_all | solution.py:127
  45.2 7.4 %copy-start.7 = (s32[1,32]{1,0:T(1,128)S(1)}, s32[1,32]{1,0:T(1,128)}, u32[]{:S(2)}) copy-start(s32[1,32]{1,0:T(1,128)} %param.8) | copy-start | bytes 388
  45.2 59.1 %all-to-all-start = ((bf16[2,256,2112]{2,0,1:T(2,128)(2,1)}), bf16[2,256,2112]{2,0,1:T(2,128)(2,1)}, u32[]{:S(2)}, u32[]{:S(2)}) async-start(bf16[2,256,2112]{2,0,1:T(2,128)(2,1)} %copy.26), calls=%async_computation | async-start | bytes 4456448 | tf_op jit(solution)/shard_map/all_to_all | solution.py:124
  122.3 4.1 %copy-start.4 = (f32[16,8,32,32]{2,3,1,0:T(8,128)S(1)}, f32[16,8,32,32]{2,3,1,0:T(8,128)}, u32[]{:S(2)}) copy-start(f32[16,8,32,32]{2,3,1,0:T(8,128)} %get-tuple-element.9) | copy-start | bytes 1572868
  126.4 1.2 copy-start.3
  127.6 1.2 copy-start.2
  128.8 1.9 copy-start.5
where the time goes:
time: 302 us; the launch traced here: 301 us
  blocking collectives  135 us (45%)
  local copies, waits for them, and re-layouts  61.3 us (20%)
  waiting for transfers between devices  46.4 us (15%)
  matrix products  32.8 us (11%)
  starting transfers between devices  17.5 us (6%)
  other arithmetic  7.18 us (2%)
    psum x1, blocking collectives, on_device(): total = lax.psum(partial_term, ('dp', 'ctx'))  75.9 us
    all_to_all x1, blocking collectives, on_device(): lax.all_to_all(dqkv_moved, 'ctx', split_axis=0, concat_axis=1, tiled=True)  59 us
    all_to_all x1, waiting for transfers between devices, on_device(): lax.all_to_all(query_key_value, 'ctx', split_axis=1, concat_axis=0, tiled...  46.4 us
    reshape x2, local copies, waits for them, and re-layouts, input_projection(): query_key_value.astype(jnp.bfloat16)  14 us
    reshape x4, local copies, waits for them, and re-layouts, split_heads(): return block.reshape(block.shape[0], block.shape[1], heads, -1)  12.3 us
    all_to_all x1, starting transfers between devices, on_device(): lax.all_to_all(d_attn, 'ctx', split_axis=1, concat_axis=0, tiled=True)  10.1 us
    dot_general x1, matrix products, final_result(): lax.dot_general(flat, query_key_value_weight, (((1,), (1,)), ((), ())), p...  8.26 us
    dot_general x1, matrix products, input_projection(): jnp.dot(normalized_frames.reshape(-1, frames.shape[2]), query_key_value_w...  7.49 us
  transfers between devices with their start and end apart: 2, of which 1 were waited for; matrix products, arithmetic and copies ran while one was open for 9% of the time, Pallas kernels for 0%

commit v1 on v0

v1 whole, which is shorter than its diff:
```python
import functools
import math

import jax
import jax.numpy as jnp
from jax import lax
from jax.experimental import pallas as pl
from jax.experimental.pallas import tpu as pltpu
from jax.sharding import PartitionSpec as P

HEADS = 8
HALF = 8
VMEM_BYTES = 48 * 1024 * 1024


def dot_nn(a, b):
    return lax.dot_general(a, b, (((1,), (0,)), ((), ())), preferred_element_type=jnp.float32)


def dot_nt(a, b):
    return lax.dot_general(a, b, (((1,), (1,)), ((), ())), preferred_element_type=jnp.float32)


def dot_tn(a, b):
    return lax.dot_general(a, b, (((0,), (0,)), ((), ())), preferred_element_type=jnp.float32)


def standardize(block):
    values = block.astype(jnp.float32)
    centered = values - jnp.mean(values, axis=-1, keepdims=True)
    inverse = lax.rsqrt(jnp.mean(centered * centered, axis=-1, keepdims=True) + 1e-05)
    return centered * inverse, inverse


def project_kernel(x_ref, gain_ref, w_ref, qkv_ref, normed):
    frames, patches, d = x_ref.shape
    inner = w_ref.shape[1] // 3
    wide = qkv_ref.shape[1] // 3
    rows = frames * HALF
    step = 4

    def norm_step(i, carry):
        xhat, _ = standardize(x_ref[pl.ds(i * step, step)])
        scaled = xhat * gain_ref[...].reshape(1, 1, d)
        for half in range(patches // HALF):
            part = scaled[:, half * HALF : (half + 1) * HALF, :].reshape(step * HALF, d)
            at = pl.multiple_of(half * rows + i * step * HALF, step * HALF)
            normed[pl.ds(at, step * HALF), :] = part.astype(jnp.bfloat16)
        return carry

    lax.fori_loop(0, frames // step, norm_step, 0)
    for block in range(frames * patches // rows):
        piece = slice(block * rows, (block + 1) * rows)
        joined = dot_nn(normed[piece, :], w_ref[...]).astype(jnp.bfloat16)
        for part in range(3):
            qkv_ref[piece, part * wide : part * wide + inner] = joined[:, part * inner : (part + 1) * inner]
            qkv_ref[piece, part * wide + inner : (part + 1) * wide] = jnp.zeros(
                (rows, wide - inner), jnp.bfloat16
            )


def attend_kernel(
    qkv_ref, d_ref, x_ref, column_ref, row_ref, gain_ref, w_ref, out_ref, partial_ref,
    bias, d_attn, d_query, d_key, d_value, joined, d_norm,
):
    frames, patches, d = x_ref.shape
    inner = w_ref.shape[1] // 3
    wide = qkv_ref.shape[1] // 3
    head = inner // HEADS
    rows = frames * HALF
    halves = patches // HALF
    scale = 1.0 / math.sqrt(head)
    bias[...] = jnp.where(column_ref[...] == row_ref[...], 0.0, -1e30)
    d_attn[:, inner:] = jnp.zeros((halves * rows, wide - inner), jnp.bfloat16)
    step = 4

    def split_step(i, carry):
        block = d_ref[pl.ds(i * step, step)].astype(jnp.float32)
        for half in range(halves):
            part = block[:, half * HALF : (half + 1) * HALF, :].reshape(step * HALF, inner)
            at = pl.multiple_of(half * rows + i * step * HALF, step * HALF)
            d_attn[pl.ds(at, step * HALF), :inner] = part.astype(jnp.bfloat16)
        return carry

    lax.fori_loop(0, frames // step, split_step, 0)

    def half_step(half, carry):
        at = pl.ds(pl.multiple_of(half * rows, rows), rows)
        done = 0
        for h in range(HEADS):
            low = (h * head) // 128 * 128
            high = min(-(-((h + 1) * head) // 128) * 128, wide)
            lanes = lax.broadcasted_iota(jnp.int32, (rows, high - low), 1) + low
            own = (lanes >= h * head) & (lanes < (h + 1) * head)

            def only(block):
                return jnp.where(own, block, jnp.zeros_like(block))

            query = only(qkv_ref[at, low:high])
            key = only(qkv_ref[at, wide + low : wide + high])
            value = qkv_ref[at, 2 * wide + low : 2 * wide + high]
            cot = only(d_attn[at, low:high])
            scores = dot_nt(key, query) * scale + bias[...]
            expo = jnp.exp(scores - jnp.max(scores, axis=0, keepdims=True))
            probs = expo * (1.0 / jnp.sum(expo, axis=0, keepdims=True))
            d_weights = dot_nt(value, cot)
            d_scores = probs * (d_weights - jnp.sum(probs * d_weights, axis=0, keepdims=True))
            d_scores = d_scores.astype(jnp.bfloat16)
            for target, found in (
                (d_query, dot_tn(d_scores, key) * scale),
                (d_key, dot_nn(d_scores, query) * scale),
                (d_value, dot_nn(probs.astype(jnp.bfloat16), cot)),
            ):
                shared = max(done - low, 0)
                if shared:
                    target[:, low:done] += found[:, :shared]
                if high > done:
                    target[:, max(low, done) : high] = found[:, shared:]
            done = high
        joined[at, 0:inner] = d_query[:, :inner].astype(jnp.bfloat16)
        joined[at, inner : 2 * inner] = d_key[:, :inner].astype(jnp.bfloat16)
        joined[at, 2 * inner :] = d_value[:, :inner].astype(jnp.bfloat16)
        d_norm[at, :] = dot_nt(joined[at, :], w_ref[...])
        return carry

    lax.fori_loop(0, halves, half_step, 0)
    partial_ref[...] = jnp.zeros_like(partial_ref)

    def back_step(i, carry):
        xhat, inverse = standardize(x_ref[pl.ds(i * step, step)])
        grads = jnp.concatenate(
            [
                d_norm[
                    pl.ds(pl.multiple_of(half * rows + i * step * HALF, step * HALF), step * HALF), :
                ].reshape(step, HALF, d)
                for half in range(halves)
            ],
            axis=1,
        )
        partial_ref[...] += jnp.sum((grads * xhat).reshape(step * patches, d), axis=0, keepdims=True)
        e = grads * gain_ref[...].reshape(1, 1, d)
        first = jnp.mean(e, axis=-1, keepdims=True)
        second = jnp.mean(e * xhat, axis=-1, keepdims=True)
        out_ref[pl.ds(i * step, step)] = (inverse * (e - first - xhat * second)).astype(jnp.bfloat16)
        return carry

    lax.fori_loop(0, frames // step, back_step, 0)


def vmem(count):
    return [pl.BlockSpec(memory_space=pltpu.VMEM)] * count


def project(x, gain, weight):
    frames, patches, d = x.shape
    inner = weight.shape[1] // 3
    wide = -(-inner // 128) * 128
    rows = frames * patches
    return pl.pallas_call(
        project_kernel,
        out_shape=jax.ShapeDtypeStruct((rows, 3 * wide), jnp.bfloat16),
        in_specs=vmem(3),
        out_specs=vmem(1)[0],
        scratch_shapes=[pltpu.VMEM((rows, d), jnp.bfloat16)],
        compiler_params=pltpu.CompilerParams(vmem_limit_bytes=VMEM_BYTES),
        cost_estimate=pl.CostEstimate(
            flops=2 * rows * d * 3 * inner, bytes_accessed=2 * (rows * d + 3 * inner * (rows + d)), transcendentals=0
        ),
        name="project",
    )(x, gain.reshape(1, d), weight)


def attend(qkv, d_attn, x, clip_row, gain, weight):
    frames, patches, d = x.shape
    inner = weight.shape[1] // 3
    wide = qkv.shape[1] // 3
    rows = frames * HALF
    total = frames * patches
    code = (clip_row[:, None] * HALF + jnp.arange(HALF, dtype=jnp.int32)[None, :]).reshape(rows)
    return pl.pallas_call(
        attend_kernel,
        out_shape=(
            jax.ShapeDtypeStruct(x.shape, jnp.bfloat16),
            jax.ShapeDtypeStruct((1, d), jnp.float32),
        ),
        in_specs=vmem(7),
        out_specs=tuple(vmem(2)),
        scratch_shapes=[
            pltpu.VMEM((rows, rows), jnp.float32),
            pltpu.VMEM((total, wide), jnp.bfloat16),
            pltpu.VMEM((rows, wide), jnp.float32),
            pltpu.VMEM((rows, wide), jnp.float32),
            pltpu.VMEM((rows, wide), jnp.float32),
            pltpu.VMEM((total, 3 * inner), jnp.bfloat16),
            pltpu.VMEM((total, d), jnp.float32),
        ],
        compiler_params=pltpu.CompilerParams(vmem_limit_bytes=VMEM_BYTES),
        cost_estimate=pl.CostEstimate(
            flops=2 * total * d * 3 * inner, bytes_accessed=2 * (total * d + 3 * inner * (total + d)), transcendentals=0
        ),
        name="attend",
    )(qkv, d_attn, x, code.reshape(rows, 1), code.reshape(1, rows), gain.reshape(1, d), weight)


def to_homes(block, members):
    frames, patches, features = block.shape
    own = patches // members
    sent = block.reshape(frames, members, own, features).transpose(1, 0, 2, 3)
    got = lax.all_to_all(sent, "ctx", 0, 0, tiled=True)
    return got.reshape(members * frames, own, features)


def to_frames(block, members):
    frames, own, features = block.shape
    got = lax.all_to_all(block.reshape(members, frames // members, own, features), "ctx", 0, 0, tiled=True)
    return got.transpose(1, 0, 2, 3).reshape(frames // members, members * own, features)


def sum_all(value, mesh_sizes):
    for axis, size in mesh_sizes:
        stride = 1
        while stride < size:
            radix = min(4, size // stride)
            moved = [value]
            for k in range(1, radix):
                pairs = [
                    (i, i - (i // stride % radix) * stride + (i // stride + k) % radix * stride)
                    for i in range(size)
                ]
                moved.append(lax.ppermute(value, axis, pairs))
            value = functools.reduce(jnp.add, moved)
            stride *= radix
    return value


def on_device(frames, cotangent, clip_ids, gain, query_key_value_weight, w_out):
    groups = lax.axis_size("dp")
    members = lax.axis_size("ctx")
    count = groups * members * frames.shape[0] * frames.shape[1]
    x = to_homes(frames, members)
    d_attn = lax.dot_general(
        cotangent.reshape(-1, cotangent.shape[2]),
        w_out,
        (((1,), (1,)), ((), ())),
        preferred_element_type=jnp.float32,
    )
    d_attn = d_attn.astype(jnp.bfloat16).reshape(cotangent.shape[:2] + (w_out.shape[0],))
    d_attn = to_homes(d_attn, members)
    qkv = project(x, gain, query_key_value_weight)
    term, partial_term = attend(qkv, d_attn, x, clip_ids[0], gain, query_key_value_weight)
    back = to_frames(term, members)
    frame_input_gradient = (cotangent.astype(jnp.float32) + back.astype(jnp.float32)).astype(jnp.bfloat16)
    total = sum_all(partial_term[0], (("dp", groups), ("ctx", members)))
    return (frame_input_gradient, total * (1.0 / math.sqrt(count)))


def solution(mesh):
    return jax.shard_map(
        on_device,
        mesh=mesh,
        in_specs=(
            P(("dp", "ctx"), None, None),
            P(("dp", "ctx"), None, None),
            P("dp", None),
            P(),
            P(),
            P(),
        ),
        out_specs=(P(("dp", "ctx"), None, None), P()),
        check_vma=False,
    )
```

time: 302 us -> 155 us (0.51)
  blocking collectives: 135 us -> 0 us
  local copies, waits for them, and re-layouts: 61.3 us -> 26.5 us
  matrix products: 32.8 us -> 3.56 us
  Pallas kernels: 0 us -> 26.3 us
  starting transfers between devices: 17.5 us -> 39.8 us
  waiting for transfers between devices: 46.4 us -> 53.7 us
  other arithmetic: 7.18 us -> 2.44 us
    psum x1 -> x0, blocking collectives: 75.9 us -> none  [on_device(): total = lax.psum(partial_term, ('dp', 'ctx'))]
    all_to_all x1 -> x0, blocking collectives: 59 us -> none  [on_device(): lax.all_to_all(dqkv_moved, 'ctx', split_axis=0, concat_axis=1, tiled=True)]
    reshape x11 -> x2, local copies, waits for them, and re-layouts: 41 us -> 4.01 us  [the longest x1 2.71 us: to_homes(): sent = block.reshape(frames, members, own, features).transpose(1, 0, 2, 3)]
    pallas_call x0 -> x2, Pallas kernels: none -> 26.3 us  [the longest x1 17.8 us: attend(): pl.pallas_call(attend_kernel, out_shape=(jax.ShapeDtypeStruct(x.shape, jn...]
    ppermute x0 -> x12, waiting for transfers between devices: none -> 25.8 us  [sum_all(): moved.append(lax.ppermute(value, axis, pairs))]
    dot_general x7 -> x1, matrix products: 28 us -> 3.56 us  [on_device(): lax.dot_general(cotangent.reshape(-1, cotangent.shape[2]), w_out, (((1,),...]
    all_to_all x2 -> x3, waiting for transfers between devices: 46.4 us -> 27.8 us  [the longest x2 27.8 us: to_homes(): got = lax.all_to_all(sent, 'ctx', 0, 0, tiled=True)]
    ppermute x0 -> x12, starting transfers between devices: none -> 18.4 us  [sum_all(): moved.append(lax.ppermute(value, axis, pairs))]
  transfers between devices with their start and end apart: 2 -> 15, of which waited for: 1 -> 8; matrix products, arithmetic and copies ran while one was open for 9% -> 13% of each run, Pallas kernels for 0% -> 5%
where the time goes in v1:
time: 155 us; the launch traced here: 153 us
  waiting for transfers between devices  53.7 us (35%)
  starting transfers between devices  39.8 us (26%)
  local copies, waits for them, and re-layouts  26.5 us (17%)
  Pallas kernels  26.3 us (17%)
  matrix products  3.56 us (2%)
  other arithmetic  2.44 us (2%)
    all_to_all x2, waiting for transfers between devices, to_homes(): got = lax.all_to_all(sent, 'ctx', 0, 0, tiled=True)  27.8 us
    ppermute x12, waiting for transfers between devices, sum_all(): moved.append(lax.ppermute(value, axis, pairs))  25.8 us
    ppermute x12, starting transfers between devices, sum_all(): moved.append(lax.ppermute(value, axis, pairs))  18.4 us
    pallas_call x1, Pallas kernels, attend(): pl.pallas_call(attend_kernel, out_shape=(jax.ShapeDtypeStruct(x.shape, jn...  17.8 us
    unnamed x23, local copies, waits for them, and re-layouts  16.4 us
    all_to_all x2, starting transfers between devices, to_homes(): got = lax.all_to_all(sent, 'ctx', 0, 0, tiled=True)  14.2 us
    pallas_call x1, Pallas kernels, project(): pl.pallas_call(project_kernel, out_shape=jax.ShapeDtypeStruct((rows, 3 *...  8.41 us
    all_to_all x1, starting transfers between devices, to_frames(): lax.all_to_all(block.reshape(members, frames // members, own, features),...  7.25 us
  transfers between devices with their start and end apart: 15, of which 8 were waited for; matrix products, arithmetic and copies ran while one was open for 13% of the time, Pallas kernels for 5%

profile of v1, /device:TPU:1, one launch (start us, length us, event | category | flops | bytes accessed | tf_op | source)
XLA Modules:
  0.0 153.0 jit_solution(10712811510648018604)
XLA Ops:
  0.6 0.0 copy-start
  0.6 2.7 %copy.28 = bf16[2,16,16,1408]{3,2,0,1:T(8,128)(2,1)} copy(bf16[2,16,16,1408]{3,2,1,0:T(8,128)(2,1)} %bitcast.25) | data formatting | bytes 2883584 | tf_op jit(solution)/shard_map/reshape | solution.py:208
  3.4 10.0 %all-to-all-start = ((bf16[16,2,16,1408]{3,2,1,0:T(8,128)(2,1)}), bf16[16,2,16,1408]{3,2,1,0:T(8,128)(2,1)S(1)}, u32[]{:S(2)}, u32[]{:S(2)}) async-start(bf16[16,2,16,1408]{3,2,1,0:T(8,128)(2,1)} %bitcast.23), calls=%async_computation | async-start | bytes 2883584 | tf_op jit(solution)/shard_map/all_to_all | solution.py:209
  13.3 0.0 copy-done
  13.3 3.6 %convolution_convert_fusion = bf16[512,704]{0,1:T(8,128)(2,1)} fusion(bf16[512,1408]{1,0:T(8,128)(2,1)} %bitcast.26, bf16[704,1408]{1,0:T(8,128)(2,1)S(1)} %copy-done), kind=kOutput, calls=%fused_computation.4 | convolution fusion | flops 1015382016 | bytes 4145152 | tf_op jit(solution)/shard_map/dot_general | solution.py:241
  16.9 2.3 %copy.22 = bf16[512,704]{1,0:T(8,128)(2,1)} copy(bf16[512,704]{0,1:T(8,128)(2,1)} %convolution_convert_fusion) | data formatting | bytes 1441792 | tf_op jit(solution)/shard_map/convert_element_type | solution.py:247
  19.2 2.1 %copy.23 = bf16[16,2,16,704]{3,2,1,0:T(8,128)(2,1)} copy(bf16[16,2,16,704]{3,2,0,1:T(8,128)(2,1)} %bitcast.24) | data formatting | bytes 1441792 | tf_op jit(solution)/shard_map/transpose | solution.py:208
  21.3 27.8 %all-to-all-done = bf16[16,2,16,1408]{3,2,1,0:T(8,128)(2,1)S(1)} async-done(((bf16[16,2,16,1408]{3,2,1,0:T(8,128)(2,1)}), bf16[16,2,16,1408]{3,2,1,0:T(8,128)(2,1)S(1)}, u32[]{:S(2)}, u32[]{:S(2)}) %all-to-all-start) | async-done | bytes 1441824 | tf_op jit(solution)/shard_map/all_to_all | solution.py:209
  49.1 4.2 %all-to-all-start.1 = ((bf16[16,2,16,704]{3,2,1,0:T(8,128)(2,1)}), bf16[16,2,16,704]{3,2,1,0:T(8,128)(2,1)}, u32[]{:S(2)}, u32[]{:S(2)}) async-start(bf16[16,2,16,704]{3,2,1,0:T(8,128)(2,1)} %copy.23), calls=%async_computation.1 | async-start | bytes 1572864 | tf_op jit(solution)/shard_map/all_to_all | solution.py:209
  53.3 0.0 copy-done.10
  53.3 0.1 iota_add_fusion
  53.4 0.0 copy-start.9
  53.4 0.6 copy-done.9
  54.0 0.7 add.76.row_ref
  54.7 0.8 add.90.column_ref
  55.5 1.3 reshape.81.gain_ref
  56.8 8.9 %copy.21.w_ref = bf16[1408,2112]{1,0:T(8,128)(2,1)} copy(bf16[1408,2112]{0,1:T(8,128)(2,1)} %param.10) | data formatting | bytes 11894784 | tf_op args[4]
  65.7 0.0 copy-start.3
  65.7 0.7 copy-done.3
  66.4 8.4 %project.1.qkv_ref = bf16[512,2304]{1,0:T(8,128)(2,1)S(1)} custom-call(bf16[32,16,1408]{2,1,0:T(8,128)(2,1)S(1)} %bitcast.21, f32[1,1408]{1,0:T(1,128)S(1)} %copy-done.3, bf16[1408,2112]{1,0:T(8,128)(2,1)} %copy.21.w_ref), custom_call_target="tpu_custom_call" | custom-call | flops 3045064704 | bytes 9551872 | tf_op jit(solution)/shard_map/project/pallas_call | solution.py:159
  74.8 0.0 copy-start.6
  74.8 1.5 copy-done.6
  76.3 0.0 all-to-all-done.1
  76.3 0.0 copy-start.4
  76.3 0.7 copy-done.4
  77.0 0.0 copy-start.5
  77.0 0.7 copy-done.5
  77.6 1.7 %copy-done.7 = bf16[512,2304]{1,0:T(8,128)(2,1)S(1)} copy-done((bf16[512,2304]{1,0:T(8,128)(2,1)S(1)}, bf16[512,2304]{1,0:T(8,128)(2,1)}, u32[]{:S(2)}) %copy-start.7) | copy-done | bytes 2359320
  79.3 17.8 %attend.1 = (bf16[32,16,1408]{2,1,0:T(8,128)(2,1)}, f32[1,1408]{1,0:T(1,128)S(1)}) custom-call(bf16[512,2304]{1,0:T(8,128)(2,1)S(1)} %copy-done.7, bf16[32,16,704]{2,1,0:T(8,128)(2,1)} %bitcast.6.d_ref, bf16[32,16,1408]{2,1,0:T(8,128)(2,1)S(1)} %bitcast.22, s32[256,1]{1,0:T(8,128)S(1)} %add.90.column_ref, s32[1,256]{1,0:T(1,128)S(1)} %copy-done.5, ...), custom_call_target="tpu_custom_call" | custom-call | flops 3045064704 | bytes 9551872 | tf_op jit(solution)/shard_map/attend/pallas_call | solution.py:180
  97.1 0.0 copy-start.1
  97.1 0.6 copy-done.1
  97.7 7.3 %all-to-all-start.2 = ((bf16[16,2,16,1408]{3,2,1,0:T(8,128)(2,1)}), bf16[16,2,16,1408]{3,2,1,0:T(8,128)(2,1)S(1)}, u32[]{:S(2)}, u32[]{:S(2)}) async-start(bf16[16,2,16,1408]{3,2,1,0:T(8,128)(2,1)} %bitcast.8), calls=%async_computation.2 | async-start | bytes 2883584 | tf_op jit(solution)/shard_map/all_to_all | solution.py:215
  105.0 0.0 copy-done.2
  105.0 2.8 %collective-permute-start.2 = (f32[1408]{0:T(1024)S(1)}, f32[1408]{0:T(1024)S(1)}, u32[]{:S(2)}, u32[]{:S(2)}) collective-permute-start(f32[1408]{0:T(1024)S(1)} %reduce), channel_id=1, source_target_pairs={{0,48},{16,0},{32,16},{48,32},{64,112},{80,64},{96,80},{112,96},{1... | collective-permute-start | bytes 16904 | tf_op jit(solution)/shard_map/ppermute | solution.py:230
  107.8 0.3 collective-permute-start.1
  108.2 0.7 collective-permute-start
  108.9 0.0 collective-permute-done.2
  108.9 3.3 %collective-permute-done.1 = f32[1408]{0:T(1024)S(1)} collective-permute-done((f32[1408]{0:T(1024)S(1)}, f32[1408]{0:T(1024)S(1)}, u32[]{:S(2)}, u32[]{:S(2)}) %collective-permute-start.1) | collective-permute-done | bytes 5664 | tf_op jit(solution)/shard_map/ppermute | solution.py:230
  112.2 0.1 collective-permute-done
  112.2 2.5 %collective-permute-start.5 = (f32[1408]{0:T(1024)S(1)}, f32[1408]{0:T(1024)S(1)}, u32[]{:S(2)}, u32[]{:S(2)}) collective-permute-start(f32[1408]{0:T(1024)S(1)} %add_add_fusion.2), channel_id=1, source_target_pairs={{0,192},{16,208},{32,224},{48,240},{64,0},{80,16},{96,32},{112,48}... | collective-permute-start | bytes 16904 | tf_op jit(solution)/shard_map/ppermute | solution.py:230
  114.7 0.5 collective-permute-start.4
  115.2 0.6 collective-permute-start.3
  115.9 0.0 collective-permute-done.5
  115.9 3.2 %collective-permute-done.4 = f32[1408]{0:T(1024)S(1)} collective-permute-done((f32[1408]{0:T(1024)S(1)}, f32[1408]{0:T(1024)S(1)}, u32[]{:S(2)}, u32[]{:S(2)}) %collective-permute-start.4) | collective-permute-done | bytes 5664 | tf_op jit(solution)/shard_map/ppermute | solution.py:230
  119.0 0.2 collective-permute-done.3
  119.3 2.9 %collective-permute-start.8 = (f32[1408]{0:T(1024)S(1)}, f32[1408]{0:T(1024)S(1)}, u32[]{:S(2)}, u32[]{:S(2)}) collective-permute-start(f32[1408]{0:T(1024)S(1)} %add_add_fusion.1), channel_id=1, source_target_pairs={{0,3},{1,0},{2,1},{3,2},{4,7},{5,4},{6,5},{7,6},{8,11},{9,8},{10,9... | collective-permute-start | bytes 16904 | tf_op jit(solution)/shard_map/ppermute | solution.py:230
  122.1 1.7 %collective-permute-start.7 = (f32[1408]{0:T(1024)S(1)}, f32[1408]{0:T(1024)S(1)}, u32[]{:S(2)}, u32[]{:S(2)}) collective-permute-start(f32[1408]{0:T(1024)S(1)} %add_add_fusion.1), channel_id=1, source_target_pairs={{0,2},{1,3},{2,0},{3,1},{4,6},{5,7},{6,4},{7,5},{8,10},{9,11},{10,... | collective-permute-start | bytes 16904 | tf_op jit(solution)/shard_map/ppermute | solution.py:230
  123.8 0.1 collective-permute-start.6
  123.9 15.2 %collective-permute-done.8 = f32[1408]{0:T(1024)S(1)} collective-permute-done((f32[1408]{0:T(1024)S(1)}, f32[1408]{0:T(1024)S(1)}, u32[]{:S(2)}, u32[]{:S(2)}) %collective-permute-start.8) | collective-permute-done | bytes 5664 | tf_op jit(solution)/shard_map/ppermute | solution.py:230
  139.1 0.0 collective-permute-done.7
  139.1 0.0 collective-permute-done.6
  139.1 2.2 %collective-permute-start.11 = (f32[1408]{0:T(1024)S(1)}, f32[1408]{0:T(1024)S(1)}, u32[]{:S(2)}, u32[]{:S(2)}) collective-permute-start(f32[1408]{0:T(1024)S(1)} %add_add_fusion), channel_id=1, source_target_pairs={{0,12},{1,13},{2,14},{3,15},{4,0},{5,1},{6,2},{7,3},{8,4},{9,5},{1... | collective-permute-start | bytes 16904 | tf_op jit(solution)/shard_map/ppermute | solution.py:230
  141.3 3.1 %collective-permute-start.10 = (f32[1408]{0:T(1024)S(1)}, f32[1408]{0:T(1024)S(1)}, u32[]{:S(2)}, u32[]{:S(2)}) collective-permute-start(f32[1408]{0:T(1024)S(1)} %add_add_fusion), channel_id=1, source_target_pairs={{0,8},{1,9},{2,10},{3,11},{4,12},{5,13},{6,14},{7,15},{8,0},{9,1},... | collective-permute-start | bytes 16904 | tf_op jit(solution)/shard_map/ppermute | solution.py:230
  144.4 1.0 collective-permute-start.9
  145.4 0.0 collective-permute-done.11
  145.4 2.3 %collective-permute-done.10 = f32[1408]{0:T(1024)S(1)} collective-permute-done((f32[1408]{0:T(1024)S(1)}, f32[1408]{0:T(1024)S(1)}, u32[]{:S(2)}, u32[]{:S(2)}) %collective-permute-start.10) | collective-permute-done | bytes 5664 | tf_op jit(solution)/shard_map/ppermute | solution.py:230
  147.7 1.6 %collective-permute-done.9 = f32[1408]{0:T(1024)S(1)} collective-permute-done((f32[1408]{0:T(1024)S(1)}, f32[1408]{0:T(1024)S(1)}, u32[]{:S(2)}, u32[]{:S(2)}) %collective-permute-start.9) | collective-permute-done | bytes 5664 | tf_op jit(solution)/shard_map/ppermute | solution.py:230
  149.3 0.6 add_multiply_fusion
  149.9 0.0 all-to-all-done.2
  149.9 0.3 convert_bitcast_fusion
  150.2 0.0 copy-start.8
  150.2 0.2 copy.26
  150.4 1.2 copy-done.8
  151.6 1.4 fusion
  (8 shorter events, 0.0 us)
Async XLA Ops:
  0.6 12.7 %copy-start = (bf16[704,1408]{1,0:T(8,128)(2,1)S(1)}, bf16[704,1408]{1,0:T(8,128)(2,1)}, u32[]{:S(2)}) copy-start(bf16[704,1408]{1,0:T(8,128)(2,1)} %param.11) | copy-start | bytes 5947396
  3.4 45.8 %all-to-all-start = ((bf16[16,2,16,1408]{3,2,1,0:T(8,128)(2,1)}), bf16[16,2,16,1408]{3,2,1,0:T(8,128)(2,1)S(1)}, u32[]{:S(2)}, u32[]{:S(2)}) async-start(bf16[16,2,16,1408]{3,2,1,0:T(8,128)(2,1)} %bitcast.23), calls=%async_computation | async-start | bytes 2883584 | tf_op jit(solution)/shard_map/all_to_all | solution.py:209
  19.2 34.1 %copy-start.10 = (s32[1,32]{1,0:T(1,128)S(1)}, s32[1,32]{1,0:T(1,128)}, u32[]{:S(2)}) copy-start(s32[1,32]{1,0:T(1,128)} %param.8) | copy-start | bytes 388
  49.1 27.1 %all-to-all-start.1 = ((bf16[16,2,16,704]{3,2,1,0:T(8,128)(2,1)}), bf16[16,2,16,704]{3,2,1,0:T(8,128)(2,1)}, u32[]{:S(2)}, u32[]{:S(2)}) async-start(bf16[16,2,16,704]{3,2,1,0:T(8,128)(2,1)} %copy.23), calls=%async_computation.1 | async-start | bytes 1572864 | tf_op jit(solution)/shard_map/all_to_all | solution.py:209
  53.4 0.6 copy-start.9
  65.7 0.7 copy-start.3
  74.8 1.5 copy-start.6
  76.3 0.7 copy-start.4
  77.0 0.7 copy-start.5
  77.6 1.7 %copy-start.7 = (bf16[512,2304]{1,0:T(8,128)(2,1)S(1)}, bf16[512,2304]{1,0:T(8,128)(2,1)}, u32[]{:S(2)}) copy-start(bf16[512,2304]{1,0:T(8,128)(2,1)} %copy-done.6) | copy-start | bytes 7077892
  97.1 0.6 copy-start.1
  97.7 7.3 %copy-start.2 = (f32[1,1408]{1,0:T(1,128)S(1)}, f32[1,1408]{1,0:T(1,128)}, u32[]{:S(2)}) copy-start(f32[1,1408]{1,0:T(1,128)} %copy-done.1) | copy-start | bytes 16900
  97.7 52.1 %all-to-all-start.2 = ((bf16[16,2,16,1408]{3,2,1,0:T(8,128)(2,1)}), bf16[16,2,16,1408]{3,2,1,0:T(8,128)(2,1)S(1)}, u32[]{:S(2)}, u32[]{:S(2)}) async-start(bf16[16,2,16,1408]{3,2,1,0:T(8,128)(2,1)} %bitcast.8), calls=%async_computation.2 | async-start | bytes 2883584 | tf_op jit(solution)/shard_map/all_to_all | solution.py:215
  105.0 3.9 %collective-permute-start.2 = (f32[1408]{0:T(1024)S(1)}, f32[1408]{0:T(1024)S(1)}, u32[]{:S(2)}, u32[]{:S(2)}) collective-permute-start(f32[1408]{0:T(1024)S(1)} %reduce), channel_id=1, source_target_pairs={{0,48},{16,0},{32,16},{48,32},{64,112},{80,64},{96,80},{112,96},{1... | collective-permute-start | bytes 16904 | tf_op jit(solution)/shard_map/ppermute | solution.py:230
  107.8 4.3 %collective-permute-start.1 = (f32[1408]{0:T(1024)S(1)}, f32[1408]{0:T(1024)S(1)}, u32[]{:S(2)}, u32[]{:S(2)}) collective-permute-start(f32[1408]{0:T(1024)S(1)} %reduce), channel_id=1, source_target_pairs={{0,32},{16,48},{32,0},{48,16},{64,96},{80,112},{96,64},{112,80},{1... | collective-permute-start | bytes 16904 | tf_op jit(solution)/shard_map/ppermute | solution.py:230
  108.2 4.0 %collective-permute-start = (f32[1408]{0:T(1024)S(1)}, f32[1408]{0:T(1024)S(1)}, u32[]{:S(2)}, u32[]{:S(2)}) collective-permute-start(f32[1408]{0:T(1024)S(1)} %reduce), channel_id=1, source_target_pairs={{0,16},{16,32},{32,48},{48,0},{64,80},{80,96},{96,112},{112,64},{1... | collective-permute-start | bytes 16904 | tf_op jit(solution)/shard_map/ppermute | solution.py:230
  112.2 3.6 %collective-permute-start.5 = (f32[1408]{0:T(1024)S(1)}, f32[1408]{0:T(1024)S(1)}, u32[]{:S(2)}, u32[]{:S(2)}) collective-permute-start(f32[1408]{0:T(1024)S(1)} %add_add_fusion.2), channel_id=1, source_target_pairs={{0,192},{16,208},{32,224},{48,240},{64,0},{80,16},{96,32},{112,48}... | collective-permute-start | bytes 16904 | tf_op jit(solution)/shard_map/ppermute | solution.py:230
  114.7 4.3 %collective-permute-start.4 = (f32[1408]{0:T(1024)S(1)}, f32[1408]{0:T(1024)S(1)}, u32[]{:S(2)}, u32[]{:S(2)}) collective-permute-start(f32[1408]{0:T(1024)S(1)} %add_add_fusion.2), channel_id=1, source_target_pairs={{0,128},{16,144},{32,160},{48,176},{64,192},{80,208},{96,224},{112... | collective-permute-start | bytes 16904 | tf_op jit(solution)/shard_map/ppermute | solution.py:230
  115.2 4.0 %collective-permute-start.3 = (f32[1408]{0:T(1024)S(1)}, f32[1408]{0:T(1024)S(1)}, u32[]{:S(2)}, u32[]{:S(2)}) collective-permute-start(f32[1408]{0:T(1024)S(1)} %add_add_fusion.2), channel_id=1, source_target_pairs={{0,64},{16,80},{32,96},{48,112},{64,128},{80,144},{96,160},{112,17... | collective-permute-start | bytes 16904 | tf_op jit(solution)/shard_map/ppermute | solution.py:230
  119.3 19.8 %collective-permute-start.8 = (f32[1408]{0:T(1024)S(1)}, f32[1408]{0:T(1024)S(1)}, u32[]{:S(2)}, u32[]{:S(2)}) collective-permute-start(f32[1408]{0:T(1024)S(1)} %add_add_fusion.1), channel_id=1, source_target_pairs={{0,3},{1,0},{2,1},{3,2},{4,7},{5,4},{6,5},{7,6},{8,11},{9,8},{10,9... | collective-permute-start | bytes 16904 | tf_op jit(solution)/shard_map/ppermute | solution.py:230
  122.1 16.9 %collective-permute-start.7 = (f32[1408]{0:T(1024)S(1)}, f32[1408]{0:T(1024)S(1)}, u32[]{:S(2)}, u32[]{:S(2)}) collective-permute-start(f32[1408]{0:T(1024)S(1)} %add_add_fusion.1), channel_id=1, source_target_pairs={{0,2},{1,3},{2,0},{3,1},{4,6},{5,7},{6,4},{7,5},{8,10},{9,11},{10,... | collective-permute-start | bytes 16904 | tf_op jit(solution)/shard_map/ppermute | solution.py:230
  123.8 15.3 %collective-permute-start.6 = (f32[1408]{0:T(1024)S(1)}, f32[1408]{0:T(1024)S(1)}, u32[]{:S(2)}, u32[]{:S(2)}) collective-permute-start(f32[1408]{0:T(1024)S(1)} %add_add_fusion.1), channel_id=1, source_target_pairs={{0,1},{1,2},{2,3},{3,0},{4,5},{5,6},{6,7},{7,4},{8,9},{9,10},{10,1... | collective-permute-start | bytes 16904 | tf_op jit(solution)/shard_map/ppermute | solution.py:230
  139.1 6.3 %collective-permute-start.11 = (f32[1408]{0:T(1024)S(1)}, f32[1408]{0:T(1024)S(1)}, u32[]{:S(2)}, u32[]{:S(2)}) collective-permute-start(f32[1408]{0:T(1024)S(1)} %add_add_fusion), channel_id=1, source_target_pairs={{0,12},{1,13},{2,14},{3,15},{4,0},{5,1},{6,2},{7,3},{8,4},{9,5},{1... | collective-permute-start | bytes 16904 | tf_op jit(solution)/shard_map/ppermute | solution.py:230
  141.3 6.4 %collective-permute-start.10 = (f32[1408]{0:T(1024)S(1)}, f32[1408]{0:T(1024)S(1)}, u32[]{:S(2)}, u32[]{:S(2)}) collective-permute-start(f32[1408]{0:T(1024)S(1)} %add_add_fusion), channel_id=1, source_target_pairs={{0,8},{1,9},{2,10},{3,11},{4,12},{5,13},{6,14},{7,15},{8,0},{9,1},... | collective-permute-start | bytes 16904 | tf_op jit(solution)/shard_map/ppermute | solution.py:230
  144.4 4.9 %collective-permute-start.9 = (f32[1408]{0:T(1024)S(1)}, f32[1408]{0:T(1024)S(1)}, u32[]{:S(2)}, u32[]{:S(2)}) collective-permute-start(f32[1408]{0:T(1024)S(1)} %add_add_fusion), channel_id=1, source_target_pairs={{0,4},{1,5},{2,6},{3,7},{4,8},{5,9},{6,10},{7,11},{8,12},{9,13},{1... | collective-permute-start | bytes 16904 | tf_op jit(solution)/shard_map/ppermute | solution.py:230
  150.2 1.4 copy-start.8

commit v2 on v0

v2 whole, which is shorter than its diff:
```python
import functools
import math

import jax
import jax.numpy as jnp
from jax import lax
from jax.experimental import pallas as pl
from jax.experimental.pallas import tpu as pltpu
from jax.sharding import PartitionSpec as P

HEADS = 8
CLIPS = 3
QUAD = 4
TILE = 8
EARLY = 3
VMEM_BYTES = 16 * 1024 * 1024
WHOLE_VMEM_BYTES = 60 * 1024 * 1024


def dot_nn(a, b):
    return lax.dot_general(a, b, (((1,), (0,)), ((), ())), preferred_element_type=jnp.float32)


def dot_nt(a, b):
    return lax.dot_general(a, b, (((1,), (1,)), ((), ())), preferred_element_type=jnp.float32)


def dot_tn(a, b):
    return lax.dot_general(a, b, (((0,), (0,)), ((), ())), preferred_element_type=jnp.float32)


def standardize(block):
    values = block.astype(jnp.float32)
    centered = values - jnp.mean(values, axis=-1, keepdims=True)
    inverse = lax.rsqrt(jnp.mean(centered * centered, axis=-1, keepdims=True) + 1e-05)
    return centered * inverse, inverse


def to_quads(first, second):
    low = lax.broadcasted_iota(jnp.int32, first.shape, 1) < QUAD
    even = jnp.where(low, first, pltpu.roll(second, QUAD, 1))
    odd = jnp.where(low, pltpu.roll(first, QUAD, 1), second)
    return even, odd


def pack_kernel(low, high, x_ref, cot_ref, w_ref, out_ref):
    _, patches, d = x_ref.shape
    homes = out_ref.shape[0] // (TILE * (high - low))

    def rows(ref):
        even, odd = to_quads(*[ref[f].astype(jnp.float32).reshape(patches // TILE, TILE, d) for f in range(2)])
        per_home = patches // homes // TILE
        found = [
            (even, odd)[q % 2][home * per_home + q // 2] for home in range(homes) for q in range(low, high)
        ]
        return jnp.concatenate(found, axis=0).astype(jnp.bfloat16)

    out_ref[:, :d] = rows(x_ref)
    out_ref[:, d:] = dot_nt(rows(cot_ref), w_ref[...]).astype(jnp.bfloat16)


def attend_kernel(
    quads, clip_ref, block, gain_ref, w_hbm, out_ref, partial_ref,
    w_ref, w_sems, standard, inverses, normed, bias, query_all, key_all, value_all, cot_all,
    probs_all, grads_all, weights_all, d_scores_all, d_query, d_key, d_value, joined, d_norm,
):
    d = w_ref.shape[1]
    inner = block.shape[1] - d
    loads = [
        pltpu.make_async_copy(
            w_hbm.at[pl.ds(part * inner, inner)], w_ref.at[pl.ds(part * inner, inner)], w_sems.at[part]
        )
        for part in range(3)
    ]
    for load in loads:
        load.start()
    wide = query_all.shape[2]
    rows = bias.shape[0]
    sources = rows // TILE
    head = inner // HEADS
    scale = 1.0 / math.sqrt(head)
    step = 8 // (1 + quads // 2)
    size = step * quads * TILE
    gains = gain_ref[...].reshape(1, d)
    frames = rows // QUAD
    begins = [sum((clip_ref[0, f] < clip).astype(jnp.int32) for f in range(frames)) for clip in range(1, CLIPS)]

    def related(dim):
        at = lax.broadcasted_iota(jnp.int32, (rows, rows), dim)
        frame, patch = at // QUAD, at % QUAD
        return sum((frame >= begin).astype(jnp.int32) for begin in begins) * QUAD + patch

    bias[...] = jnp.where(related(0) == related(1), 0.0, -1e30)

    def norm_step(i, carry):
        at = pl.ds(pl.multiple_of(i * size, size), size)
        xhat, inverse = standardize(block[at, :d])
        standard[at, :] = xhat
        inverses[at, :] = jnp.broadcast_to(inverse, (size, 128))
        normed[at, :] = (xhat * gains).astype(jnp.bfloat16)
        return carry

    lax.fori_loop(0, sources // step, norm_step, 0)

    def spread(target, found):
        found = found.reshape(sources, quads * TILE, inner)
        for q in range(quads):
            part = found[:, q * TILE : (q + 1) * TILE, :].reshape(rows, inner)
            target[q, :, :inner] = part.astype(jnp.bfloat16)
            target[q, :, inner:] = jnp.zeros((rows, wide - inner), jnp.bfloat16)

    for part, target in enumerate((query_all, key_all, value_all)):
        loads[part].wait()
        spread(target, dot_nt(normed[...], w_ref[part * inner : (part + 1) * inner, :]))
    spread(cot_all, block[:, d:].astype(jnp.float32))

    spans = []
    for h in range(HEADS):
        low = (h * head) // 128 * 128
        spans.append((low, min(-(-((h + 1) * head) // 128) * 128, wide)))

    def only(h, values):
        lanes = lax.broadcasted_iota(jnp.int32, values.shape, 1) + spans[h][0]
        return jnp.where((lanes >= h * head) & (lanes < (h + 1) * head), values, jnp.zeros_like(values))

    def quad_step(q, carry):
        for h, (low, high) in enumerate(spans):
            probs_all[h] = dot_nt(key_all[q, :, low:high], only(h, query_all[q, :, low:high]))
            grads_all[h] = dot_nt(value_all[q, :, low:high], only(h, cot_all[q, :, low:high]))
        for h in range(HEADS):
            scores = probs_all[h] * scale + bias[...]
            expo = jnp.exp(scores - jnp.max(scores, axis=0, keepdims=True))
            probs = expo * (1.0 / jnp.sum(expo, axis=0, keepdims=True))
            weights_all[h] = probs.astype(jnp.bfloat16)
            d_weights = grads_all[h]
            d_scores = probs * (d_weights - jnp.sum(probs * d_weights, axis=0, keepdims=True))
            d_scores_all[h] = d_scores.astype(jnp.bfloat16)
        at = pl.ds(pl.multiple_of(q * rows, rows), rows)
        for part, target in enumerate((d_query, d_key, d_value)):
            done = 0
            for h, (low, high) in enumerate(spans):
                if part == 0:
                    found = dot_tn(d_scores_all[h], only(h, key_all[q, :, low:high])) * scale
                elif part == 1:
                    found = dot_nn(d_scores_all[h], only(h, query_all[q, :, low:high])) * scale
                else:
                    found = dot_nn(weights_all[h], only(h, cot_all[q, :, low:high]))
                shared = max(done - low, 0)
                if shared:
                    target[:, low:done] += found[:, :shared]
                if high > done:
                    target[:, max(low, done) : high] = found[:, shared:]
                done = high
            joined[at, part * inner : (part + 1) * inner] = target[:, :inner].astype(jnp.bfloat16)
        return carry

    lax.fori_loop(0, quads, quad_step, 0)
    d_norm[...] = dot_nn(joined[...], w_ref[...]).reshape(quads, rows, d)
    partial_ref[...] = jnp.zeros_like(partial_ref)

    def back_step(i, carry):
        at = pl.ds(pl.multiple_of(i * size, size), size)
        xhat = standard[at, :]
        inverse = inverses[at, :1]
        found = d_norm[:, pl.ds(pl.multiple_of(i * step * TILE, step * TILE), step * TILE), :]
        grads = jnp.concatenate(
            [found[q, s * TILE : (s + 1) * TILE] for s in range(step) for q in range(quads)], axis=0
        )
        partial_ref[...] += jnp.sum(grads * xhat, axis=0, keepdims=True)
        e = grads * gains
        first = jnp.mean(e, axis=-1, keepdims=True)
        second = jnp.mean(e * xhat, axis=-1, keepdims=True)
        term = inverse * (e - first - xhat * second)
        out_ref[at, :] = term.astype(jnp.bfloat16)
        return carry

    lax.fori_loop(0, sources // step, back_step, 0)


def finish_kernel(cot_ref, early_ref, late_ref, out_ref, sum_ref):
    _, patches, d = cot_ref.shape
    late_rows = late_ref.shape[0]
    homes = late_rows // TILE
    early = early_ref[...].astype(jnp.float32).reshape(homes, -1, d)
    late = late_ref[...].astype(jnp.float32).reshape(homes, TILE, -1)
    term = jnp.concatenate([early, late[:, :, :d]], axis=1).reshape(patches // TILE, 2 * TILE, d)
    terms = to_quads(term[:, :TILE], term[:, TILE:])
    for f in range(2):
        total = cot_ref[f].astype(jnp.float32) + terms[f].reshape(patches, d)
        out_ref[f] = total.astype(jnp.bfloat16)

    @pl.when(pl.program_id(0) == 0)
    def _():
        sum_ref[...] = jnp.zeros_like(sum_ref)

    sum_ref[...] += jnp.sum(late[:, :, d:], axis=0)


def vmem(count):
    return [pl.BlockSpec(memory_space=pltpu.VMEM)] * count


def params(limit):
    return pltpu.CompilerParams(vmem_limit_bytes=limit)


def pack(low, high, frames, cotangent, w_out, members):
    each, patches, d = frames.shape
    inner = w_out.shape[0]
    steps = 2
    rows = members * (high - low) * TILE
    tokens = pl.BlockSpec((each, patches // steps, d), lambda i: (0, i, 0))
    return pl.pallas_call(
        functools.partial(pack_kernel, low, high),
        grid=(steps,),
        out_shape=jax.ShapeDtypeStruct((rows, d + inner), jnp.bfloat16),
        in_specs=[tokens, tokens, pl.BlockSpec((inner, d), lambda i: (0, 0))],
        out_specs=pl.BlockSpec((rows // steps, d + inner), lambda i: (i, 0)),
        compiler_params=params(WHOLE_VMEM_BYTES),
        cost_estimate=pl.CostEstimate(
            flops=2 * rows * d * inner, bytes_accessed=2 * (d * inner + 4 * rows * d), transcendentals=0
        ),
        name=f"pack_{low}",
    )(frames, cotangent, w_out)


def attend(block, clip_ids, gain, weight):
    d = weight.shape[1]
    inner = weight.shape[0] // 3
    wide = -(-inner // 128) * 128
    rows = clip_ids.shape[1] * QUAD
    quads = block.shape[0] // rows
    bf16, f32 = jnp.bfloat16, jnp.float32
    return pl.pallas_call(
        functools.partial(attend_kernel, quads),
        out_shape=(jax.ShapeDtypeStruct((quads * rows, d), bf16), jax.ShapeDtypeStruct((1, d), f32)),
        in_specs=[pl.BlockSpec(memory_space=pltpu.SMEM)] + vmem(2) + [pl.BlockSpec(memory_space=pl.ANY)],
        out_specs=tuple(vmem(2)),
        scratch_shapes=[pltpu.VMEM((3 * inner, d), bf16), pltpu.SemaphoreType.DMA((3,))]
        + [pltpu.VMEM((quads * rows, d), f32), pltpu.VMEM((quads * rows, 128), f32)]
        + [pltpu.VMEM((quads * rows, d), bf16), pltpu.VMEM((rows, rows), f32)]
        + [pltpu.VMEM((quads, rows, wide), bf16)] * 4
        + [pltpu.VMEM((HEADS, rows, rows), f32)] * 2
        + [pltpu.VMEM((HEADS, rows, rows), bf16)] * 2
        + [pltpu.VMEM((rows, wide), f32)] * 3
        + [pltpu.VMEM((quads * rows, 3 * inner), bf16), pltpu.VMEM((quads, rows, d), f32)],
        compiler_params=params(WHOLE_VMEM_BYTES),
        cost_estimate=pl.CostEstimate(flops=0, bytes_accessed=0, transcendentals=0),
        name=f"attend_{quads}",
    )(clip_ids, block, gain, weight)


def finish(cotangent, early, late):
    each, patches, d = cotangent.shape
    steps = 4
    tokens = pl.BlockSpec((each, patches // steps, d), lambda i: (0, i, 0))
    extra = late.shape[1] - d
    return pl.pallas_call(
        finish_kernel,
        grid=(steps,),
        out_shape=(
            jax.ShapeDtypeStruct(cotangent.shape, jnp.bfloat16),
            jax.ShapeDtypeStruct((TILE, extra), jnp.float32),
        ),
        in_specs=[tokens]
        + [pl.BlockSpec((rows.shape[0] // steps, rows.shape[1]), lambda i: (i, 0)) for rows in (early, late)],
        out_specs=(tokens, pl.BlockSpec((TILE, extra), lambda i: (0, 0))),
        compiler_params=params(VMEM_BYTES),
        name="finish",
    )(cotangent, early, late)


def ride(vector):
    high = lax.reduce_precision(vector, 8, 7)
    top, rest = high.reshape(-1, 128), (vector - high).reshape(-1, 128)
    over = top.shape[0] - TILE
    gap = jnp.zeros((TILE - 2 * over, 128), jnp.float32)
    middle = jnp.concatenate([top[TILE:], rest[TILE:], gap], axis=0)
    return jnp.concatenate([top[:TILE], middle, rest[:TILE]], axis=1).astype(jnp.bfloat16)


def alight(found, size):
    over = size // 128 - TILE
    first, middle, last = found[:, :128], found[:, 128:256], found[:, 256:]
    return jnp.concatenate([first + last, middle[:over] + middle[over : 2 * over]], axis=0).reshape(size)


def to_all(block):
    return lax.all_to_all(block, "ctx", 0, 0, tiled=True)


def on_device(frames, cotangent, clip_ids, gain, query_key_value_weight, w_out):
    groups = lax.axis_size("dp")
    members = lax.axis_size("ctx")
    count = groups * members * frames.shape[0] * frames.shape[1]
    d = frames.shape[2]
    quads = frames.shape[1] // members // QUAD
    weight = query_key_value_weight.T
    early = to_all(pack(0, EARLY, frames, cotangent, w_out, members))
    late = pack(EARLY, quads, frames, cotangent, w_out, members)
    early, late = lax.optimization_barrier((early, late))
    late = to_all(late)
    early_term, early_partial = attend(early, clip_ids, gain, weight)
    early_back = to_all(early_term)
    late_term, late_partial = attend(late, clip_ids, gain, weight)
    over_groups = ride(jnp.sum(lax.all_gather(early_partial + late_partial, "dp"), axis=0) * (1.0 / math.sqrt(count)))
    late_term = jnp.concatenate([late_term, jnp.tile(over_groups, (members, 1))], axis=1)
    early_back, late_term = lax.optimization_barrier((early_back, late_term))
    frame_input_gradient, total = finish(cotangent, early_back, to_all(late_term))
    return (frame_input_gradient, alight(total, d))


def solution(mesh):
    return jax.shard_map(
        on_device,
        mesh=mesh,
        in_specs=(
            P(("dp", "ctx"), None, None),
            P(("dp", "ctx"), None, None),
            P("dp", None),
            P(),
            P(),
            P(),
        ),
        out_specs=(P(("dp", "ctx"), None, None), P()),
        check_vma=False,
    )
```

time: 302 us -> 143 us (0.47)
  blocking collectives: 135 us -> 46.9 us
  local copies, waits for them, and re-layouts: 61.3 us -> 0.09 us
  Pallas kernels: 0 us -> 34.6 us
  matrix products: 32.8 us -> 0 us
  waiting for transfers between devices: 46.4 us -> 39.1 us
  other arithmetic: 7.18 us -> 2.53 us
    psum x1 -> x0, blocking collectives: 75.9 us -> none  [on_device(): total = lax.psum(partial_term, ('dp', 'ctx'))]
    reshape x11 -> x0, local copies, waits for them, and re-layouts: 41 us -> none  [the longest x2 14 us: input_projection(): query_key_value.astype(jnp.bfloat16)]
    pallas_call x0 -> x5, Pallas kernels: none -> 34.6 us  [the longest x2 23.3 us: attend(): pl.pallas_call(functools.partial(attend_kernel, quads), out_shape=(jax.Sh...]
    all_to_all x1, blocking collectives: 59 us -> 27.3 us  [to_all(): return lax.all_to_all(block, 'ctx', 0, 0, tiled=True)]
    dot_general x7 -> x0, matrix products: 28 us -> none  [the longest x1 8.26 us: final_result(): lax.dot_general(flat, query_key_value_weight, (((1,), (1,)), ((), ())), p...]
    all_gather x0 -> x1, blocking collectives: none -> 19.7 us  [on_device(): lax.all_gather(early_partial + late_partial, 'dp')]
    all_to_all x2 -> x3, waiting for transfers between devices: 46.4 us -> 39.1 us  [to_all(): return lax.all_to_all(block, 'ctx', 0, 0, tiled=True)]
    convert_element_type x3 -> x0, other arithmetic: 5.7 us -> none  [the longest x1 4.48 us: final_result(): frame_input_gradient = (cotangent.astype(jnp.float32) + norm_backward(nor...]
  transfers between devices with their start and end apart: 2 -> 3, of which waited for: 1 -> 2; matrix products, arithmetic and copies ran while one was open for 9% -> 1% of each run, Pallas kernels for 0% -> 19%
where the time goes in v2:
time: 143 us
  blocking collectives  46.9 us (33%)
  waiting for transfers between devices  39.1 us (27%)
  Pallas kernels  34.6 us (24%)
  starting transfers between devices  18.7 us (13%)
  other arithmetic  2.53 us (2%)
    all_to_all x3, waiting for transfers between devices, to_all(): return lax.all_to_all(block, 'ctx', 0, 0, tiled=True)  39.1 us
    all_to_all x1, blocking collectives, to_all(): return lax.all_to_all(block, 'ctx', 0, 0, tiled=True)  27.3 us
    pallas_call x2, Pallas kernels, attend(): pl.pallas_call(functools.partial(attend_kernel, quads), out_shape=(jax.Sh...  23.3 us
    all_gather x1, blocking collectives, on_device(): lax.all_gather(early_partial + late_partial, 'dp')  19.7 us
    all_to_all x3, starting transfers between devices, to_all(): return lax.all_to_all(block, 'ctx', 0, 0, tiled=True)  18.7 us
    pallas_call x2, Pallas kernels, pack(): pl.pallas_call(functools.partial(pack_kernel, low, high), grid=(steps,),...  9.21 us
  transfers between devices with their start and end apart: 3, of which 2 were waited for; matrix products, arithmetic and copies ran while one was open for 1% of the time, Pallas kernels for 19%

profile of v2, /device:TPU:1, one launch (start us, length us, event | category | flops | bytes accessed | tf_op | source)
XLA Modules:
  0.0 142.7 jit_solution(13923903486908561724)
XLA Ops:
  0.6 5.0 %pack_0.1 = bf16[384,2112]{1,0:T(8,128)(2,1)} custom-call(bf16[2,256,1408]{2,1,0:T(8,128)(2,1)} %x_ref.3, bf16[2,256,1408]{2,1,0:T(8,128)(2,1)} %cot_ref.5, bf16[704,1408]{1,0:T(8,128)(2,1)} %w_ref.3), custom_call_target="tpu_custom_call" | custom-call | flops 761266176 | bytes 6307840 | tf_op jit(solution)/shard_map/pack_0/pallas_call | solution.py:213
  5.6 10.0 %all-to-all-start = ((bf16[16,24,2112]{2,1,0:T(8,128)(2,1)}), bf16[16,24,2112]{2,1,0:T(8,128)(2,1)S(1)}, u32[]{:S(2)}, u32[]{:S(2)}) async-start(bf16[16,24,2112]{2,1,0:T(8,128)(2,1)} %bitcast.24), calls=%async_computation | async-start | bytes 3342336 | tf_op jit(solution)/shard_map/all_to_all | solution.py:289
  15.6 4.2 %pack_3.1 = bf16[128,2112]{1,0:T(8,128)(2,1)} custom-call(bf16[2,256,1408]{2,1,0:T(8,128)(2,1)} %x_ref.3, bf16[2,256,1408]{2,1,0:T(8,128)(2,1)} %cot_ref.5, bf16[704,1408]{1,0:T(8,128)(2,1)} %w_ref.3), custom_call_target="tpu_custom_call" | custom-call | flops 253755392 | bytes 3424256 | tf_op jit(solution)/shard_map/pack_3/pallas_call | solution.py:213
  19.8 36.2 %all-to-all-done = bf16[16,24,2112]{2,1,0:T(8,128)(2,1)S(1)} async-done(((bf16[16,24,2112]{2,1,0:T(8,128)(2,1)}), bf16[16,24,2112]{2,1,0:T(8,128)(2,1)S(1)}, u32[]{:S(2)}, u32[]{:S(2)}) %all-to-all-start) | async-done | bytes 1622048 | tf_op jit(solution)/shard_map/all_to_all | solution.py:289
  56.0 0.0 copy-start.1
  56.0 4.4 %all-to-all-start.2 = ((bf16[16,8,2112]{2,1,0:T(8,128)(2,1)}), bf16[16,8,2112]{2,1,0:T(8,128)(2,1)S(1)}, u32[]{:S(2)}, u32[]{:S(2)}) async-start(bf16[16,8,2112]{2,1,0:T(8,128)(2,1)} %bitcast.26), calls=%async_computation.2 | async-start | bytes 1114112 | tf_op jit(solution)/shard_map/all_to_all | solution.py:289
  60.4 0.0 copy-done.1
  60.4 15.1 %attend_3.1 = (bf16[384,1408]{1,0:T(8,128)(2,1)}, f32[1,1408]{1,0:T(1,128)}) custom-call(s32[1,32]{1,0:T(1,128)} %clip_ref.3, bf16[384,2112]{1,0:T(8,128)(2,1)} %bitcast.23, f32[1408]{0:T(1024)} %gain_ref.3, bf16[2112,1408]{1,0:T(8,128)(2,1)} %bitcast.21), custom_call_target="tpu_custom_call" | custom-call | tf_op jit(solution)/shard_map/attend_3/pallas_call | solution.py:234
  75.5 2.9 %all-to-all-done.2 = bf16[16,8,2112]{2,1,0:T(8,128)(2,1)S(1)} async-done(((bf16[16,8,2112]{2,1,0:T(8,128)(2,1)}), bf16[16,8,2112]{2,1,0:T(8,128)(2,1)S(1)}, u32[]{:S(2)}, u32[]{:S(2)}) %all-to-all-start.2) | async-done | bytes 540704 | tf_op jit(solution)/shard_map/all_to_all | solution.py:289
  78.4 0.0 copy-start.2
  78.4 4.3 %all-to-all-start.1 = ((bf16[16,24,1408]{2,1,0:T(8,128)(2,1)}), bf16[16,24,1408]{2,1,0:T(8,128)(2,1)S(1)}, u32[]{:S(2)}, u32[]{:S(2)}) async-start(bf16[16,24,1408]{2,1,0:T(8,128)(2,1)} %bitcast.28), calls=%async_computation.1 | async-start | bytes 2162688 | tf_op jit(solution)/shard_map/all_to_all | solution.py:289
  82.7 0.0 copy-done.2
  82.7 0.0 copy-start.3
  82.7 8.2 %attend_1.1 = (bf16[128,1408]{1,0:T(8,128)(2,1)}, f32[1,1408]{1,0:T(1,128)}) custom-call(s32[1,32]{1,0:T(1,128)} %clip_ref.3, bf16[128,2112]{1,0:T(8,128)(2,1)} %bitcast.25, f32[1408]{0:T(1024)} %gain_ref.3, bf16[2112,1408]{1,0:T(8,128)(2,1)} %bitcast.22), custom_call_target="tpu_custom_call" | custom-call | tf_op jit(solution)/shard_map/attend_1/pallas_call | solution.py:234
  90.9 0.0 copy-start
  91.0 0.0 copy-done.3
  91.0 0.8 add_bitcast_fusion
  91.8 19.7 %all-gather.1 = f32[16,1,1408]{2,1,0:T(1,128)S(1)} all-gather(f32[1,1,1408]{2,1,0:T(1,128)S(1)} %add_bitcast_fusion), channel_id=2, replica_groups=mesh['dp'=16,'ctx'=16] {'dp'}, dimensions={0}, use_global_device_ids=true | all-gather | bytes 95744 | tf_op jit(solution)/shard_map/all_gather | solution.py:306
  111.4 0.1 reduce.1
  111.7 1.0 pad_maximum_fusion
  112.7 0.0 all-to-all-done.1
  112.7 27.3 %all_to_all.46 = bf16[16,8,1792]{2,1,0:T(8,128)(2,1)S(1)} all-to-all(bf16[16,8,1792]{2,1,0:T(8,128)(2,1)S(1)} %bitcast.27), channel_id=1, replica_groups=mesh['dp'=16,'ctx'=16] {'ctx'}, dimensions={0} | all-to-all | bytes 917504 | tf_op jit(solution)/shard_map/all_to_all | solution.py:289
  139.9 0.0 copy-done
  139.9 2.1 %finish.1 = (bf16[2,256,1408]{2,1,0:T(8,128)(2,1)}, f32[8,384]{1,0:T(8,128)S(1)}) custom-call(bf16[2,256,1408]{2,1,0:T(8,128)(2,1)S(1)} %copy-done, bf16[384,1408]{1,0:T(8,128)(2,1)S(1)} %bitcast.19, bf16[128,1792]{1,0:T(8,128)(2,1)S(1)} %bitcast.20), custom_call_target="tpu_custom_call" | custom-call | tf_op jit(solution)/shard_map/finish/pallas_call | solution.py:258
  142.1 0.6 maximum_bitcast_fusion
  (9 shorter events, 0.1 us)
Async XLA Ops:
  5.6 50.4 %all-to-all-start = ((bf16[16,24,2112]{2,1,0:T(8,128)(2,1)}), bf16[16,24,2112]{2,1,0:T(8,128)(2,1)S(1)}, u32[]{:S(2)}, u32[]{:S(2)}) async-start(bf16[16,24,2112]{2,1,0:T(8,128)(2,1)} %bitcast.24), calls=%async_computation | async-start | bytes 3342336 | tf_op jit(solution)/shard_map/all_to_all | solution.py:289
  56.0 4.4 %copy-start.1 = (bf16[16,24,2112]{2,1,0:T(8,128)(2,1)}, bf16[16,24,2112]{2,1,0:T(8,128)(2,1)S(1)}, u32[]{:S(2)}) copy-start(bf16[16,24,2112]{2,1,0:T(8,128)(2,1)S(1)} %all-to-all-done) | copy-start | bytes 4866052
  56.0 22.4 %all-to-all-start.2 = ((bf16[16,8,2112]{2,1,0:T(8,128)(2,1)}), bf16[16,8,2112]{2,1,0:T(8,128)(2,1)S(1)}, u32[]{:S(2)}, u32[]{:S(2)}) async-start(bf16[16,8,2112]{2,1,0:T(8,128)(2,1)} %bitcast.26), calls=%async_computation.2 | async-start | bytes 1114112 | tf_op jit(solution)/shard_map/all_to_all | solution.py:289
  78.4 4.3 %copy-start.2 = (bf16[16,8,2112]{2,1,0:T(8,128)(2,1)}, bf16[16,8,2112]{2,1,0:T(8,128)(2,1)S(1)}, u32[]{:S(2)}) copy-start(bf16[16,8,2112]{2,1,0:T(8,128)(2,1)S(1)} %all-to-all-done.2) | copy-start | bytes 1622020
  78.4 34.3 %all-to-all-start.1 = ((bf16[16,24,1408]{2,1,0:T(8,128)(2,1)}), bf16[16,24,1408]{2,1,0:T(8,128)(2,1)S(1)}, u32[]{:S(2)}, u32[]{:S(2)}) async-start(bf16[16,24,1408]{2,1,0:T(8,128)(2,1)} %bitcast.28), calls=%async_computation.1 | async-start | bytes 2162688 | tf_op jit(solution)/shard_map/all_to_all | solution.py:289
  82.7 8.2 %copy-start.3 = (f32[1,1408]{1,0:T(1,128)S(1)}, f32[1,1408]{1,0:T(1,128)}, u32[]{:S(2)}) copy-start(f32[1,1408]{1,0:T(1,128)} %get-tuple-element.16) | copy-start | bytes 16900
  90.9 49.0 %copy-start = (bf16[2,256,1408]{2,1,0:T(8,128)(2,1)S(1)}, bf16[2,256,1408]{2,1,0:T(8,128)(2,1)}, u32[]{:S(2)}) copy-start(bf16[2,256,1408]{2,1,0:T(8,128)(2,1)} %cot_ref.5) | copy-start | bytes 4325380

commit v3 on v2

--- a/solution.py
+++ b/solution.py
@@ -12,6 +12,8 @@
 CLIPS = 3
 QUAD = 4
 TILE = 8
+PIECES = 4
+RIDER = 384
 EARLY = 3
 VMEM_BYTES = 16 * 1024 * 1024
 WHOLE_VMEM_BYTES = 60 * 1024 * 1024
@@ -60,17 +62,16 @@
 
 
 def attend_kernel(
-    quads, clip_ref, block, gain_ref, w_hbm, out_ref, partial_ref,
+    quads, clip_ref, block, gain_ref, before_ref, w_hbm, out_ref, partial_ref,
     w_ref, w_sems, standard, inverses, normed, bias, query_all, key_all, value_all, cot_all,
     probs_all, grads_all, weights_all, d_scores_all, d_query, d_key, d_value, joined, d_norm,
 ):
     d = w_ref.shape[1]
     inner = block.shape[1] - d
+    piece = inner // PIECES
     loads = [
-        pltpu.make_async_copy(
-            w_hbm.at[pl.ds(part * inner, inner)], w_ref.at[pl.ds(part * inner, inner)], w_sems.at[part]
-        )
-        for part in range(3)
+        pltpu.make_async_copy(w_hbm.at[pl.ds(k * piece, piece)], w_ref.at[pl.ds(k * piece, piece)], w_sems.at[k])
+        for k in range(3 * PIECES)
     ]
     for load in loads:
         load.start()
@@ -110,7 +111,8 @@
             target[q, :, inner:] = jnp.zeros((rows, wide - inner), jnp.bfloat16)
 
     for part, target in enumerate((query_all, key_all, value_all)):
-        loads[part].wait()
+        for load in loads[part * PIECES : (part + 1) * PIECES]:
+            load.wait()
         spread(target, dot_nt(normed[...], w_ref[part * inner : (part + 1) * inner, :]))
     spread(cot_all, block[:, d:].astype(jnp.float32))
 
@@ -156,7 +158,10 @@
 
     lax.fori_loop(0, quads, quad_step, 0)
     d_norm[...] = dot_nn(joined[...], w_ref[...]).reshape(quads, rows, d)
-    partial_ref[...] = jnp.zeros_like(partial_ref)
+    partial_ref[...] = before_ref[...]
+    extra = out_ref.shape[1] - d
+    if extra:
+        out_ref[:, d:] = jnp.zeros((out_ref.shape[0], extra), jnp.bfloat16)
 
     def back_step(i, carry):
         at = pl.ds(pl.multiple_of(i * size, size), size)
@@ -171,7 +176,7 @@
         first = jnp.mean(e, axis=-1, keepdims=True)
         second = jnp.mean(e * xhat, axis=-1, keepdims=True)
         term = inverse * (e - first - xhat * second)
-        out_ref[at, :] = term.astype(jnp.bfloat16)
+        out_ref[at, :d] = term.astype(jnp.bfloat16)
         return carry
 
     lax.fori_loop(0, sources // step, back_step, 0)
@@ -224,7 +229,7 @@
     )(frames, cotangent, w_out)
 
 
-def attend(block, clip_ids, gain, weight):
+def attend(block, clip_ids, gain, weight, before, extra):
     d = weight.shape[1]
     inner = weight.shape[0] // 3
     wide = -(-inner // 128) * 128
@@ -233,10 +238,10 @@
     bf16, f32 = jnp.bfloat16, jnp.float32
     return pl.pallas_call(
         functools.partial(attend_kernel, quads),
-        out_shape=(jax.ShapeDtypeStruct((quads * rows, d), bf16), jax.ShapeDtypeStruct((1, d), f32)),
-        in_specs=[pl.BlockSpec(memory_space=pltpu.SMEM)] + vmem(2) + [pl.BlockSpec(memory_space=pl.ANY)],
+        out_shape=(jax.ShapeDtypeStruct((quads * rows, d + extra), bf16), jax.ShapeDtypeStruct((1, d), f32)),
+        in_specs=[pl.BlockSpec(memory_space=pltpu.SMEM)] + vmem(3) + [pl.BlockSpec(memory_space=pl.ANY)],
         out_specs=tuple(vmem(2)),
-        scratch_shapes=[pltpu.VMEM((3 * inner, d), bf16), pltpu.SemaphoreType.DMA((3,))]
+        scratch_shapes=[pltpu.VMEM((3 * inner, d), bf16), pltpu.SemaphoreType.DMA((3 * PIECES,))]
         + [pltpu.VMEM((quads * rows, d), f32), pltpu.VMEM((quads * rows, 128), f32)]
         + [pltpu.VMEM((quads * rows, d), bf16), pltpu.VMEM((rows, rows), f32)]
         + [pltpu.VMEM((quads, rows, wide), bf16)] * 4
@@ -247,7 +252,7 @@
         compiler_params=params(WHOLE_VMEM_BYTES),
         cost_estimate=pl.CostEstimate(flops=0, bytes_accessed=0, transcendentals=0),
         name=f"attend_{quads}",
-    )(clip_ids, block, gain, weight)
+    )(clip_ids, block, gain, before, weight)
 
 
 def finish(cotangent, early, late):
@@ -289,6 +294,16 @@
     return lax.all_to_all(block, "ctx", 0, 0, tiled=True)
 
 
+def sum_groups(value, groups):
+    side = math.isqrt(groups)
+    if side * side != groups:
+        return lax.psum(value, "dp")
+    rows = [[i * side + j for j in range(side)] for i in range(side)]
+    value = lax.psum(value, "dp", axis_index_groups=rows)
+    moved = [lax.ppermute(value, "dp", [(i, (i + k * side) % groups) for i in range(groups)]) for k in range(1, side)]
+    return functools.reduce(jnp.add, moved, value)
+
+
 def on_device(frames, cotangent, clip_ids, gain, query_key_value_weight, w_out):
     groups = lax.axis_size("dp")
     members = lax.axis_size("ctx")
@@ -300,11 +315,11 @@
     late = pack(EARLY, quads, frames, cotangent, w_out, members)
     early, late = lax.optimization_barrier((early, late))
     late = to_all(late)
-    early_term, early_partial = attend(early, clip_ids, gain, weight)
+    early_term, partial_term = attend(early, clip_ids, gain, weight, jnp.zeros((1, d), jnp.float32), 0)
     early_back = to_all(early_term)
-    late_term, late_partial = attend(late, clip_ids, gain, weight)
-    over_groups = ride(jnp.sum(lax.all_gather(early_partial + late_partial, "dp"), axis=0) * (1.0 / math.sqrt(count)))
-    late_term = jnp.concatenate([late_term, jnp.tile(over_groups, (members, 1))], axis=1)
+    late_term, partial_term = attend(late, clip_ids, gain, weight, partial_term, RIDER)
+    rider = ride(sum_groups(partial_term, groups) * (1.0 / math.sqrt(count)))
+    late_term = lax.dynamic_update_slice(late_term, jnp.tile(rider, (members, 1)), (0, d))
     early_back, late_term = lax.optimization_barrier((early_back, late_term))
     frame_input_gradient, total = finish(cotangent, early_back, to_all(late_term))
     return (frame_input_gradient, alight(total, d))

time: 143 us -> 138 us (0.965)
  blocking collectives: 46.9 us -> 32.3 us
  starting transfers between devices: 18.7 us -> 24.2 us
  waiting for transfers between devices: 39.1 us -> 43.4 us
  other arithmetic: 2.53 us -> 0.65 us
    all_gather x1 -> x0, blocking collectives: 19.7 us -> none  [on_device(): lax.all_gather(early_partial + late_partial, 'dp')]
    psum x0 -> x1, blocking collectives: none -> 9.56 us  [sum_groups(): value = lax.psum(value, 'dp', axis_index_groups=rows)]
    ppermute x0 -> x3, starting transfers between devices: none -> 4.9 us  [sum_groups(): lax.ppermute(value, 'dp', [(i, (i + k * side) % groups) for i in range(gr...]
    all_to_all x1, blocking collectives: 27.3 us -> 22.7 us  [to_all(): return lax.all_to_all(block, 'ctx', 0, 0, tiled=True)]
    all_to_all x3, waiting for transfers between devices: 39.1 us -> 41.8 us  [to_all(): return lax.all_to_all(block, 'ctx', 0, 0, tiled=True)]
    ppermute x0 -> x3, waiting for transfers between devices: none -> 1.61 us  [sum_groups(): lax.ppermute(value, 'dp', [(i, (i + k * side) % groups) for i in range(gr...]
  transfers between devices with their start and end apart: 3 -> 6, of which waited for: 2 -> 5; matrix products, arithmetic and copies ran while one was open for 1% -> 1% of each run, Pallas kernels for 19% -> 20%
where the time goes in v3:
time: 138 us; the launch traced here: 137 us
  waiting for transfers between devices  43.4 us (31%)
  Pallas kernels  34.8 us (25%)
  blocking collectives  32.3 us (23%)
  starting transfers between devices  24.2 us (18%)
    all_to_all x3, waiting for transfers between devices, to_all(): return lax.all_to_all(block, 'ctx', 0, 0, tiled=True)  41.8 us
    pallas_call x2, Pallas kernels, attend(): pl.pallas_call(functools.partial(attend_kernel, quads), out_shape=(jax.Sh...  23.4 us
    all_to_all x1, blocking collectives, to_all(): return lax.all_to_all(block, 'ctx', 0, 0, tiled=True)  22.7 us
    all_to_all x3, starting transfers between devices, to_all(): return lax.all_to_all(block, 'ctx', 0, 0, tiled=True)  19.3 us
    psum x1, blocking collectives, sum_groups(): value = lax.psum(value, 'dp', axis_index_groups=rows)  9.56 us
    pallas_call x2, Pallas kernels, pack(): pl.pallas_call(functools.partial(pack_kernel, low, high), grid=(steps,),...  9.21 us
    ppermute x3, starting transfers between devices, sum_groups(): lax.ppermute(value, 'dp', [(i, (i + k * side) % groups) for i in range(gr...  4.9 us
  transfers between devices with their start and end apart: 6, of which 5 were waited for; matrix products, arithmetic and copies ran while one was open for 1% of the time, Pallas kernels for 20%

profile of v3, /device:TPU:1, one launch (start us, length us, event | category | flops | bytes accessed | tf_op | source)
XLA Modules:
  0.0 137.4 jit_solution(1902099911673997945)
XLA Ops:
  0.6 5.0 %pack_0.1 = bf16[384,2112]{1,0:T(8,128)(2,1)} custom-call(bf16[2,256,1408]{2,1,0:T(8,128)(2,1)} %x_ref.3, bf16[2,256,1408]{2,1,0:T(8,128)(2,1)} %cot_ref.5, bf16[704,1408]{1,0:T(8,128)(2,1)} %w_ref.3), custom_call_target="tpu_custom_call" | custom-call | flops 761266176 | bytes 6307840 | tf_op jit(solution)/shard_map/pack_0/pallas_call | solution.py:218
  5.6 10.0 %all-to-all-start = ((bf16[16,24,2112]{2,1,0:T(8,128)(2,1)}), bf16[16,24,2112]{2,1,0:T(8,128)(2,1)S(1)}, u32[]{:S(2)}, u32[]{:S(2)}) async-start(bf16[16,24,2112]{2,1,0:T(8,128)(2,1)} %bitcast.22), calls=%async_computation | async-start | bytes 3342336 | tf_op jit(solution)/shard_map/all_to_all | solution.py:294
  15.6 4.2 %pack_3.1 = bf16[128,2112]{1,0:T(8,128)(2,1)} custom-call(bf16[2,256,1408]{2,1,0:T(8,128)(2,1)} %x_ref.3, bf16[2,256,1408]{2,1,0:T(8,128)(2,1)} %cot_ref.5, bf16[704,1408]{1,0:T(8,128)(2,1)} %w_ref.3), custom_call_target="tpu_custom_call" | custom-call | flops 253755392 | bytes 3424256 | tf_op jit(solution)/shard_map/pack_3/pallas_call | solution.py:218
  19.8 36.2 %all-to-all-done = bf16[16,24,2112]{2,1,0:T(8,128)(2,1)S(1)} async-done(((bf16[16,24,2112]{2,1,0:T(8,128)(2,1)}), bf16[16,24,2112]{2,1,0:T(8,128)(2,1)S(1)}, u32[]{:S(2)}, u32[]{:S(2)}) %all-to-all-start) | async-done | bytes 1622048 | tf_op jit(solution)/shard_map/all_to_all | solution.py:294
  56.0 0.0 copy-start.1
  56.0 4.4 %all-to-all-start.2 = ((bf16[16,8,2112]{2,1,0:T(8,128)(2,1)}), bf16[16,8,2112]{2,1,0:T(8,128)(2,1)S(1)}, u32[]{:S(2)}, u32[]{:S(2)}) async-start(bf16[16,8,2112]{2,1,0:T(8,128)(2,1)} %bitcast.24), calls=%async_computation.2 | async-start | bytes 1114112 | tf_op jit(solution)/shard_map/all_to_all | solution.py:294
  60.4 0.6 broadcast_in_dim.6.before_ref
  61.0 0.0 copy-done.1
  61.0 15.0 %attend_3.1 = (bf16[384,1408]{1,0:T(8,128)(2,1)}, f32[1,1408]{1,0:T(1,128)}) custom-call(s32[1,32]{1,0:T(1,128)} %clip_ref.3, bf16[384,2112]{1,0:T(8,128)(2,1)} %bitcast.21, f32[1408]{0:T(1024)} %gain_ref.3, f32[1,1408]{1,0:T(1,128)} %broadcast_in_dim.6.before_ref, bf16[2112,1408]{1,0:T(8,128)(2,1)} %bitcast.19), custom_call_target="tpu_custom_call" | custom-call | tf_op jit(solution)/shard_map/attend_3/pallas_call | solution.py:239
  76.0 2.3 %all-to-all-done.2 = bf16[16,8,2112]{2,1,0:T(8,128)(2,1)S(1)} async-done(((bf16[16,8,2112]{2,1,0:T(8,128)(2,1)}), bf16[16,8,2112]{2,1,0:T(8,128)(2,1)S(1)}, u32[]{:S(2)}, u32[]{:S(2)}) %all-to-all-start.2) | async-done | bytes 540704 | tf_op jit(solution)/shard_map/all_to_all | solution.py:294
  78.4 0.0 copy-start.2
  78.4 5.0 %all-to-all-start.1 = ((bf16[16,24,1408]{2,1,0:T(8,128)(2,1)}), bf16[16,24,1408]{2,1,0:T(8,128)(2,1)S(1)}, u32[]{:S(2)}, u32[]{:S(2)}) async-start(bf16[16,24,1408]{2,1,0:T(8,128)(2,1)} %bitcast.25), calls=%async_computation.1 | async-start | bytes 2162688 | tf_op jit(solution)/shard_map/all_to_all | solution.py:294
  83.3 0.0 copy-done.2
  83.3 0.0 copy-start
  83.3 8.4 %attend_1.1 = (bf16[128,1792]{1,0:T(8,128)(2,1)}, f32[1,1408]{1,0:T(1,128)}) custom-call(s32[1,32]{1,0:T(1,128)} %clip_ref.3, bf16[128,2112]{1,0:T(8,128)(2,1)} %bitcast.23, f32[1408]{0:T(1024)} %gain_ref.3, f32[1,1408]{1,0:T(1,128)} %get-tuple-element.15.before_ref, bf16[2112,1408]{1,0:T(8,128)(2,1)} %bitcast.20), custom_call_target="tpu_custom_call" | custom-call | tf_op jit(solution)/shard_map/attend_1/pallas_call | solution.py:239
  91.7 9.6 %psum.7 = f32[1,1408]{1,0:T(1,128)S(1)} all-reduce(f32[1,1408]{1,0:T(1,128)} %get-tuple-element.17), channel_id=1, replica_groups={{0,16,32,48},{64,80,96,112},{128,144,160,176},{192,208,224,240},{1,17,3..., use_global_device_ids=true, to_apply=%region_0.0 | all-reduce | flops 1408 | bytes 11264 | tf_op jit(solution)/shard_map/psum | solution.py:302
  101.3 1.3 collective-permute-start
  102.6 2.4 %collective-permute-start.1 = (f32[1,1408]{1,0:T(1,128)S(1)}, f32[1,1408]{1,0:T(1,128)S(1)}, u32[]{:S(2)}, u32[]{:S(2)}) collective-permute-start(f32[1,1408]{1,0:T(1,128)S(1)} %psum.7), channel_id=1, source_target_pairs={{0,128},{16,144},{32,160},{48,176},{64,192},{80,208},{96,224},{112... | collective-permute-start | bytes 16904 | tf_op jit(solution)/shard_map/ppermute | solution.py:303
  105.0 1.2 collective-permute-start.2
  106.2 0.0 collective-permute-done
  106.2 0.4 collective-permute-done.1
  106.6 1.2 collective-permute-done.2
  108.0 0.7 bitcast_dynamic-update-slice_fusion
  108.6 3.3 %all-to-all-done.1 = bf16[16,24,1408]{2,1,0:T(8,128)(2,1)S(1)} async-done(((bf16[16,24,1408]{2,1,0:T(8,128)(2,1)}), bf16[16,24,1408]{2,1,0:T(8,128)(2,1)S(1)}, u32[]{:S(2)}, u32[]{:S(2)}) %all-to-all-start.1) | async-done | bytes 1081376 | tf_op jit(solution)/shard_map/all_to_all | solution.py:294
  111.9 22.7 %all_to_all.46 = bf16[16,8,1792]{2,1,0:T(8,128)(2,1)S(1)} all-to-all(bf16[16,8,1792]{2,1,0:T(8,128)(2,1)} %bitcast.26), channel_id=1, replica_groups=mesh['dp'=16,'ctx'=16] {'ctx'}, dimensions={0} | all-to-all | bytes 917504 | tf_op jit(solution)/shard_map/all_to_all | solution.py:294
  134.6 0.0 copy-done
  134.6 2.1 %finish.1 = (bf16[2,256,1408]{2,1,0:T(8,128)(2,1)}, f32[8,384]{1,0:T(8,128)S(1)}) custom-call(bf16[2,256,1408]{2,1,0:T(8,128)(2,1)S(1)} %copy-done, bf16[384,1408]{1,0:T(8,128)(2,1)S(1)} %bitcast.17, bf16[128,1792]{1,0:T(8,128)(2,1)S(1)} %bitcast.18), custom_call_target="tpu_custom_call" | custom-call | tf_op jit(solution)/shard_map/finish/pallas_call | solution.py:263
  136.8 0.6 maximum_bitcast_fusion
  (10 shorter events, 0.1 us)
Async XLA Ops:
  5.6 50.4 %all-to-all-start = ((bf16[16,24,2112]{2,1,0:T(8,128)(2,1)}), bf16[16,24,2112]{2,1,0:T(8,128)(2,1)S(1)}, u32[]{:S(2)}, u32[]{:S(2)}) async-start(bf16[16,24,2112]{2,1,0:T(8,128)(2,1)} %bitcast.22), calls=%async_computation | async-start | bytes 3342336 | tf_op jit(solution)/shard_map/all_to_all | solution.py:294
  56.0 5.0 %copy-start.1 = (bf16[16,24,2112]{2,1,0:T(8,128)(2,1)}, bf16[16,24,2112]{2,1,0:T(8,128)(2,1)S(1)}, u32[]{:S(2)}) copy-start(bf16[16,24,2112]{2,1,0:T(8,128)(2,1)S(1)} %all-to-all-done) | copy-start | bytes 4866052
  56.0 22.4 %all-to-all-start.2 = ((bf16[16,8,2112]{2,1,0:T(8,128)(2,1)}), bf16[16,8,2112]{2,1,0:T(8,128)(2,1)S(1)}, u32[]{:S(2)}, u32[]{:S(2)}) async-start(bf16[16,8,2112]{2,1,0:T(8,128)(2,1)} %bitcast.24), calls=%async_computation.2 | async-start | bytes 1114112 | tf_op jit(solution)/shard_map/all_to_all | solution.py:294
  78.4 5.0 %copy-start.2 = (bf16[16,8,2112]{2,1,0:T(8,128)(2,1)}, bf16[16,8,2112]{2,1,0:T(8,128)(2,1)S(1)}, u32[]{:S(2)}) copy-start(bf16[16,8,2112]{2,1,0:T(8,128)(2,1)S(1)} %all-to-all-done.2) | copy-start | bytes 1622020
  78.4 33.5 %all-to-all-start.1 = ((bf16[16,24,1408]{2,1,0:T(8,128)(2,1)}), bf16[16,24,1408]{2,1,0:T(8,128)(2,1)S(1)}, u32[]{:S(2)}, u32[]{:S(2)}) async-start(bf16[16,24,1408]{2,1,0:T(8,128)(2,1)} %bitcast.25), calls=%async_computation.1 | async-start | bytes 2162688 | tf_op jit(solution)/shard_map/all_to_all | solution.py:294
  83.3 51.3 %copy-start = (bf16[2,256,1408]{2,1,0:T(8,128)(2,1)S(1)}, bf16[2,256,1408]{2,1,0:T(8,128)(2,1)}, u32[]{:S(2)}) copy-start(bf16[2,256,1408]{2,1,0:T(8,128)(2,1)} %cot_ref.5) | copy-start | bytes 4325380
  101.3 4.9 %collective-permute-start = (f32[1,1408]{1,0:T(1,128)S(1)}, f32[1,1408]{1,0:T(1,128)S(1)}, u32[]{:S(2)}, u32[]{:S(2)}) collective-permute-start(f32[1,1408]{1,0:T(1,128)S(1)} %psum.7), channel_id=1, source_target_pairs={{0,64},{16,80},{32,96},{48,112},{64,128},{80,144},{96,160},{112,17... | collective-permute-start | bytes 16904 | tf_op jit(solution)/shard_map/ppermute | solution.py:303
  102.6 4.0 %collective-permute-start.1 = (f32[1,1408]{1,0:T(1,128)S(1)}, f32[1,1408]{1,0:T(1,128)S(1)}, u32[]{:S(2)}, u32[]{:S(2)}) collective-permute-start(f32[1,1408]{1,0:T(1,128)S(1)} %psum.7), channel_id=1, source_target_pairs={{0,128},{16,144},{32,160},{48,176},{64,192},{80,208},{96,224},{112... | collective-permute-start | bytes 16904 | tf_op jit(solution)/shard_map/ppermute | solution.py:303
  105.0 2.8 %collective-permute-start.2 = (f32[1,1408]{1,0:T(1,128)S(1)}, f32[1,1408]{1,0:T(1,128)S(1)}, u32[]{:S(2)}, u32[]{:S(2)}) collective-permute-start(f32[1,1408]{1,0:T(1,128)S(1)} %psum.7), channel_id=1, source_target_pairs={{0,192},{16,208},{32,224},{48,240},{64,0},{80,16},{96,32},{112,48}... | collective-permute-start | bytes 16904 | tf_op jit(solution)/shard_map/ppermute | solution.py:303

commit v4 on v3

--- a/solution.py
+++ b/solution.py
@@ -61,10 +61,14 @@
     out_ref[:, d:] = dot_nt(rows(cot_ref), w_ref[...]).astype(jnp.bfloat16)
 
 
+def late_kernel(quads, clip_ref, block, gain_ref, w_hbm, before_ref, *refs):
+    attend_kernel(quads, clip_ref, block, gain_ref, w_hbm, *refs, before_ref=before_ref)
+
+
 def attend_kernel(
-    quads, clip_ref, block, gain_ref, before_ref, w_hbm, out_ref, partial_ref,
+    quads, clip_ref, block, gain_ref, w_hbm, out_ref, partial_ref,
     w_ref, w_sems, standard, inverses, normed, bias, query_all, key_all, value_all, cot_all,
-    probs_all, grads_all, weights_all, d_scores_all, d_query, d_key, d_value, joined, d_norm,
+    probs_all, grads_all, weights_all, d_scores_all, d_query, d_key, d_value, joined, d_norm, before_ref=None,
 ):
     d = w_ref.shape[1]
     inner = block.shape[1] - d
@@ -110,12 +114,11 @@
             target[q, :, :inner] = part.astype(jnp.bfloat16)
             target[q, :, inner:] = jnp.zeros((rows, wide - inner), jnp.bfloat16)
 
+    spread(cot_all, block[:, d:].astype(jnp.float32))
     for part, target in enumerate((query_all, key_all, value_all)):
         for load in loads[part * PIECES : (part + 1) * PIECES]:
             load.wait()
         spread(target, dot_nt(normed[...], w_ref[part * inner : (part + 1) * inner, :]))
-    spread(cot_all, block[:, d:].astype(jnp.float32))
-
     spans = []
     for h in range(HEADS):
         low = (h * head) // 128 * 128
@@ -158,7 +161,7 @@
 
     lax.fori_loop(0, quads, quad_step, 0)
     d_norm[...] = dot_nn(joined[...], w_ref[...]).reshape(quads, rows, d)
-    partial_ref[...] = before_ref[...]
+    partial_ref[...] = jnp.zeros_like(partial_ref) if before_ref is None else before_ref[...]
     extra = out_ref.shape[1] - d
     if extra:
         out_ref[:, d:] = jnp.zeros((out_ref.shape[0], extra), jnp.bfloat16)
@@ -182,7 +185,7 @@
     lax.fori_loop(0, sources // step, back_step, 0)
 
 
-def finish_kernel(cot_ref, early_ref, late_ref, out_ref, sum_ref):
+def finish_kernel(cot_ref, early_ref, late_ref, out_ref, sum_ref, rider):
     _, patches, d = cot_ref.shape
     late_rows = late_ref.shape[0]
     homes = late_rows // TILE
@@ -196,9 +199,19 @@
 
     @pl.when(pl.program_id(0) == 0)
     def _():
-        sum_ref[...] = jnp.zeros_like(sum_ref)
-
-    sum_ref[...] += jnp.sum(late[:, :, d:], axis=0)
+        rider[...] = jnp.zeros_like(rider)
+
+    rider[...] += jnp.sum(late[:, :, d:], axis=0)
+
+    @pl.when(pl.program_id(0) == pl.num_programs(0) - 1)
+    def _():
+        over = d // 128 - TILE
+        for row in range(d // 128):
+            if row < TILE:
+                both = rider[row, :128] + rider[row, 256:]
+            else:
+                both = rider[row - TILE, 128:256] + rider[row - TILE + over, 128:256]
+            sum_ref[row * 128 : (row + 1) * 128] = both
 
 
 def vmem(count):
@@ -229,17 +242,18 @@
     )(frames, cotangent, w_out)
 
 
-def attend(block, clip_ids, gain, weight, before, extra):
+def attend(block, clip_ids, gain, weight, before=None, extra=0):
     d = weight.shape[1]
     inner = weight.shape[0] // 3
     wide = -(-inner // 128) * 128
     rows = clip_ids.shape[1] * QUAD
     quads = block.shape[0] // rows
     bf16, f32 = jnp.bfloat16, jnp.float32
+    more = [] if before is None else [before]
     return pl.pallas_call(
-        functools.partial(attend_kernel, quads),
+        functools.partial(late_kernel if more else attend_kernel, quads),
         out_shape=(jax.ShapeDtypeStruct((quads * rows, d + extra), bf16), jax.ShapeDtypeStruct((1, d), f32)),
-        in_specs=[pl.BlockSpec(memory_space=pltpu.SMEM)] + vmem(3) + [pl.BlockSpec(memory_space=pl.ANY)],
+        in_specs=[pl.BlockSpec(memory_space=pltpu.SMEM)] + vmem(2) + [pl.BlockSpec(memory_space=pl.ANY)] + vmem(len(more)),
         out_specs=tuple(vmem(2)),
         scratch_shapes=[pltpu.VMEM((3 * inner, d), bf16), pltpu.SemaphoreType.DMA((3 * PIECES,))]
         + [pltpu.VMEM((quads * rows, d), f32), pltpu.VMEM((quads * rows, 128), f32)]
@@ -252,12 +266,12 @@
         compiler_params=params(WHOLE_VMEM_BYTES),
         cost_estimate=pl.CostEstimate(flops=0, bytes_accessed=0, transcendentals=0),
         name=f"attend_{quads}",
-    )(clip_ids, block, gain, before, weight)
+    )(clip_ids, block, gain, weight, *more)
 
 
 def finish(cotangent, early, late):
     each, patches, d = cotangent.shape
-    steps = 4
+    steps = 2
     tokens = pl.BlockSpec((each, patches // steps, d), lambda i: (0, i, 0))
     extra = late.shape[1] - d
     return pl.pallas_call(
@@ -265,11 +279,12 @@
         grid=(steps,),
         out_shape=(
             jax.ShapeDtypeStruct(cotangent.shape, jnp.bfloat16),
-            jax.ShapeDtypeStruct((TILE, extra), jnp.float32),
+            jax.ShapeDtypeStruct((d,), jnp.float32),
         ),
         in_specs=[tokens]
         + [pl.BlockSpec((rows.shape[0] // steps, rows.shape[1]), lambda i: (i, 0)) for rows in (early, late)],
-        out_specs=(tokens, pl.BlockSpec((TILE, extra), lambda i: (0, 0))),
+        out_specs=(tokens, pl.BlockSpec((d,), lambda i: (0,))),
+        scratch_shapes=[pltpu.VMEM((TILE, extra), jnp.float32)],
         compiler_params=params(VMEM_BYTES),
         name="finish",
     )(cotangent, early, late)
@@ -282,12 +297,6 @@
     gap = jnp.zeros((TILE - 2 * over, 128), jnp.float32)
     middle = jnp.concatenate([top[TILE:], rest[TILE:], gap], axis=0)
     return jnp.concatenate([top[:TILE], middle, rest[:TILE]], axis=1).astype(jnp.bfloat16)
-
-
-def alight(found, size):
-    over = size // 128 - TILE
-    first, middle, last = found[:, :128], found[:, 128:256], found[:, 256:]
-    return jnp.concatenate([first + last, middle[:over] + middle[over : 2 * over]], axis=0).reshape(size)
 
 
 def to_all(block):
@@ -315,14 +324,13 @@
     late = pack(EARLY, quads, frames, cotangent, w_out, members)
     early, late = lax.optimization_barrier((early, late))
     late = to_all(late)
-    early_term, partial_term = attend(early, clip_ids, gain, weight, jnp.zeros((1, d), jnp.float32), 0)
+    early_term, partial_term = attend(early, clip_ids, gain, weight)
     early_back = to_all(early_term)
     late_term, partial_term = attend(late, clip_ids, gain, weight, partial_term, RIDER)
     rider = ride(sum_groups(partial_term, groups) * (1.0 / math.sqrt(count)))
     late_term = lax.dynamic_update_slice(late_term, jnp.tile(rider, (members, 1)), (0, d))
     early_back, late_term = lax.optimization_barrier((early_back, late_term))
-    frame_input_gradient, total = finish(cotangent, early_back, to_all(late_term))
-    return (frame_input_gradient, alight(total, d))
+    return finish(cotangent, early_back, to_all(late_term))
 
 
 def solution(mesh):

time: 138 us -> 136 us (0.986)
  no operation moved by 1% of the time
where the time goes in v4:
time: 136 us
  waiting for transfers between devices  43.8 us (32%)
  Pallas kernels  34.3 us (25%)
  blocking collectives  32.5 us (24%)
  starting transfers between devices  23.8 us (18%)
    all_to_all x3, waiting for transfers between devices, to_all(): return lax.all_to_all(block, 'ctx', 0, 0, tiled=True)  42.2 us
    pallas_call x2, Pallas kernels, attend(): pl.pallas_call(functools.partial(late_kernel if more else attend_kernel,...  23.4 us
    all_to_all x1, blocking collectives, to_all(): return lax.all_to_all(block, 'ctx', 0, 0, tiled=True)  22.9 us
    all_to_all x3, starting transfers between devices, to_all(): return lax.all_to_all(block, 'ctx', 0, 0, tiled=True)  18.7 us
    psum x1, blocking collectives, sum_groups(): value = lax.psum(value, 'dp', axis_index_groups=rows)  9.56 us
    pallas_call x2, Pallas kernels, pack(): pl.pallas_call(functools.partial(pack_kernel, low, high), grid=(steps,),...  9.2 us
    ppermute x3, starting transfers between devices, sum_groups(): lax.ppermute(value, 'dp', [(i, (i + k * side) % groups) for i in range(gr...  5.08 us
  transfers between devices with their start and end apart: 6, of which 5 were waited for; matrix products, arithmetic and copies ran while one was open for 1% of the time, Pallas kernels for 20%

profile of v4, /device:TPU:1, one launch (start us, length us, event | category | flops | bytes accessed | tf_op | source)
XLA Modules:
  0.0 135.9 jit_solution(15864989799307546498)
XLA Ops:
  0.6 5.0 %pack_0.1 = bf16[384,2112]{1,0:T(8,128)(2,1)} custom-call(bf16[2,256,1408]{2,1,0:T(8,128)(2,1)} %x_ref.3, bf16[2,256,1408]{2,1,0:T(8,128)(2,1)} %cot_ref.5, bf16[704,1408]{1,0:T(8,128)(2,1)} %w_ref.3), custom_call_target="tpu_custom_call" | custom-call | flops 761266176 | bytes 6307840 | tf_op jit(solution)/shard_map/pack_0/pallas_call | solution.py:231
  5.6 10.0 %all-to-all-start = ((bf16[16,24,2112]{2,1,0:T(8,128)(2,1)}), bf16[16,24,2112]{2,1,0:T(8,128)(2,1)S(1)}, u32[]{:S(2)}, u32[]{:S(2)}) async-start(bf16[16,24,2112]{2,1,0:T(8,128)(2,1)} %bitcast.20), calls=%async_computation | async-start | bytes 3342336 | tf_op jit(solution)/shard_map/all_to_all | solution.py:303
  15.6 4.3 %pack_3.1 = bf16[128,2112]{1,0:T(8,128)(2,1)} custom-call(bf16[2,256,1408]{2,1,0:T(8,128)(2,1)} %x_ref.3, bf16[2,256,1408]{2,1,0:T(8,128)(2,1)} %cot_ref.5, bf16[704,1408]{1,0:T(8,128)(2,1)} %w_ref.3), custom_call_target="tpu_custom_call" | custom-call | flops 253755392 | bytes 3424256 | tf_op jit(solution)/shard_map/pack_3/pallas_call | solution.py:231
  19.8 36.2 %all-to-all-done = bf16[16,24,2112]{2,1,0:T(8,128)(2,1)S(1)} async-done(((bf16[16,24,2112]{2,1,0:T(8,128)(2,1)}), bf16[16,24,2112]{2,1,0:T(8,128)(2,1)S(1)}, u32[]{:S(2)}, u32[]{:S(2)}) %all-to-all-start) | async-done | bytes 1622048 | tf_op jit(solution)/shard_map/all_to_all | solution.py:303
  56.0 0.0 copy-start.1
  56.0 4.4 %all-to-all-start.2 = ((bf16[16,8,2112]{2,1,0:T(8,128)(2,1)}), bf16[16,8,2112]{2,1,0:T(8,128)(2,1)S(1)}, u32[]{:S(2)}, u32[]{:S(2)}) async-start(bf16[16,8,2112]{2,1,0:T(8,128)(2,1)} %bitcast.22), calls=%async_computation.2 | async-start | bytes 1114112 | tf_op jit(solution)/shard_map/all_to_all | solution.py:303
  60.4 0.0 copy-done.1
  60.4 15.0 %attend_3.1 = (bf16[384,1408]{1,0:T(8,128)(2,1)}, f32[1,1408]{1,0:T(1,128)}) custom-call(s32[1,32]{1,0:T(1,128)} %clip_ref.3, bf16[384,2112]{1,0:T(8,128)(2,1)} %bitcast.19, f32[1408]{0:T(1024)} %gain_ref.3, bf16[2112,1408]{1,0:T(8,128)(2,1)} %bitcast.17), custom_call_target="tpu_custom_call" | custom-call | tf_op jit(solution)/shard_map/attend_3/pallas_call | solution.py:253
  75.4 2.9 %all-to-all-done.2 = bf16[16,8,2112]{2,1,0:T(8,128)(2,1)S(1)} async-done(((bf16[16,8,2112]{2,1,0:T(8,128)(2,1)}), bf16[16,8,2112]{2,1,0:T(8,128)(2,1)S(1)}, u32[]{:S(2)}, u32[]{:S(2)}) %all-to-all-start.2) | async-done | bytes 540704 | tf_op jit(solution)/shard_map/all_to_all | solution.py:303
  78.3 0.0 copy-start.2
  78.3 4.3 %all-to-all-start.1 = ((bf16[16,24,1408]{2,1,0:T(8,128)(2,1)}), bf16[16,24,1408]{2,1,0:T(8,128)(2,1)S(1)}, u32[]{:S(2)}, u32[]{:S(2)}) async-start(bf16[16,24,1408]{2,1,0:T(8,128)(2,1)} %bitcast.23), calls=%async_computation.1 | async-start | bytes 2162688 | tf_op jit(solution)/shard_map/all_to_all | solution.py:303
  82.7 0.0 copy-done.2
  82.7 0.0 copy-start
  82.7 8.4 %attend_1.1 = (bf16[128,1792]{1,0:T(8,128)(2,1)}, f32[1,1408]{1,0:T(1,128)}) custom-call(s32[1,32]{1,0:T(1,128)} %clip_ref.3, bf16[128,2112]{1,0:T(8,128)(2,1)} %bitcast.21, f32[1408]{0:T(1024)} %gain_ref.3, bf16[2112,1408]{1,0:T(8,128)(2,1)} %bitcast.18, f32[1,1408]{1,0:T(1,128)} %get-tuple-element.13.before_ref), custom_call_target="tpu_custom_call" | custom-call | tf_op jit(solution)/shard_map/attend_1/pallas_call | solution.py:253
  91.1 9.6 %psum.7 = f32[1,1408]{1,0:T(1,128)S(1)} all-reduce(f32[1,1408]{1,0:T(1,128)} %get-tuple-element.15), channel_id=1, replica_groups={{0,16,32,48},{64,80,96,112},{128,144,160,176},{192,208,224,240},{1,17,3..., use_global_device_ids=true, to_apply=%region_0.0 | all-reduce | flops 1408 | bytes 11264 | tf_op jit(solution)/shard_map/psum | solution.py:311
  100.7 1.5 %collective-permute-start = (f32[1,1408]{1,0:T(1,128)S(1)}, f32[1,1408]{1,0:T(1,128)S(1)}, u32[]{:S(2)}, u32[]{:S(2)}) collective-permute-start(f32[1,1408]{1,0:T(1,128)S(1)} %psum.7), channel_id=1, source_target_pairs={{0,64},{16,80},{32,96},{48,112},{64,128},{80,144},{96,160},{112,17... | collective-permute-start | bytes 16904 | tf_op jit(solution)/shard_map/ppermute | solution.py:312
  102.1 2.4 %collective-permute-start.1 = (f32[1,1408]{1,0:T(1,128)S(1)}, f32[1,1408]{1,0:T(1,128)S(1)}, u32[]{:S(2)}, u32[]{:S(2)}) collective-permute-start(f32[1,1408]{1,0:T(1,128)S(1)} %psum.7), channel_id=1, source_target_pairs={{0,128},{16,144},{32,160},{48,176},{64,192},{80,208},{96,224},{112... | collective-permute-start | bytes 16904 | tf_op jit(solution)/shard_map/ppermute | solution.py:312
  104.6 1.2 collective-permute-start.2
  105.7 0.0 collective-permute-done
  105.7 0.4 collective-permute-done.1
  106.1 1.2 collective-permute-done.2
  107.5 0.7 bitcast_dynamic-update-slice_fusion
  108.2 3.1 %all-to-all-done.1 = bf16[16,24,1408]{2,1,0:T(8,128)(2,1)S(1)} async-done(((bf16[16,24,1408]{2,1,0:T(8,128)(2,1)}), bf16[16,24,1408]{2,1,0:T(8,128)(2,1)S(1)}, u32[]{:S(2)}, u32[]{:S(2)}) %all-to-all-start.1) | async-done | bytes 1081376 | tf_op jit(solution)/shard_map/all_to_all | solution.py:303
  111.3 22.9 %all_to_all.46 = bf16[16,8,1792]{2,1,0:T(8,128)(2,1)S(1)} all-to-all(bf16[16,8,1792]{2,1,0:T(8,128)(2,1)} %bitcast.24), channel_id=1, replica_groups=mesh['dp'=16,'ctx'=16] {'ctx'}, dimensions={0} | all-to-all | bytes 917504 | tf_op jit(solution)/shard_map/all_to_all | solution.py:303
  134.2 0.0 copy-done
  134.2 1.7 %finish.1 = (bf16[2,256,1408]{2,1,0:T(8,128)(2,1)}, f32[1408]{0:T(1024)}) custom-call(bf16[2,256,1408]{2,1,0:T(8,128)(2,1)S(1)} %copy-done, bf16[384,1408]{1,0:T(8,128)(2,1)S(1)} %bitcast.15, bf16[128,1792]{1,0:T(8,128)(2,1)S(1)} %bitcast.16), custom_call_target="tpu_custom_call" | custom-call | tf_op jit(solution)/shard_map/finish/pallas_call | solution.py:277
  (8 shorter events, 0.1 us)
Async XLA Ops:
  5.6 50.4 %all-to-all-start = ((bf16[16,24,2112]{2,1,0:T(8,128)(2,1)}), bf16[16,24,2112]{2,1,0:T(8,128)(2,1)S(1)}, u32[]{:S(2)}, u32[]{:S(2)}) async-start(bf16[16,24,2112]{2,1,0:T(8,128)(2,1)} %bitcast.20), calls=%async_computation | async-start | bytes 3342336 | tf_op jit(solution)/shard_map/all_to_all | solution.py:303
  56.0 4.4 %copy-start.1 = (bf16[16,24,2112]{2,1,0:T(8,128)(2,1)}, bf16[16,24,2112]{2,1,0:T(8,128)(2,1)S(1)}, u32[]{:S(2)}) copy-start(bf16[16,24,2112]{2,1,0:T(8,128)(2,1)S(1)} %all-to-all-done) | copy-start | bytes 4866052
  56.0 22.4 %all-to-all-start.2 = ((bf16[16,8,2112]{2,1,0:T(8,128)(2,1)}), bf16[16,8,2112]{2,1,0:T(8,128)(2,1)S(1)}, u32[]{:S(2)}, u32[]{:S(2)}) async-start(bf16[16,8,2112]{2,1,0:T(8,128)(2,1)} %bitcast.22), calls=%async_computation.2 | async-start | bytes 1114112 | tf_op jit(solution)/shard_map/all_to_all | solution.py:303
  78.3 4.3 %copy-start.2 = (bf16[16,8,2112]{2,1,0:T(8,128)(2,1)}, bf16[16,8,2112]{2,1,0:T(8,128)(2,1)S(1)}, u32[]{:S(2)}) copy-start(bf16[16,8,2112]{2,1,0:T(8,128)(2,1)S(1)} %all-to-all-done.2) | copy-start | bytes 1622020
  78.3 32.9 %all-to-all-start.1 = ((bf16[16,24,1408]{2,1,0:T(8,128)(2,1)}), bf16[16,24,1408]{2,1,0:T(8,128)(2,1)S(1)}, u32[]{:S(2)}, u32[]{:S(2)}) async-start(bf16[16,24,1408]{2,1,0:T(8,128)(2,1)} %bitcast.23), calls=%async_computation.1 | async-start | bytes 2162688 | tf_op jit(solution)/shard_map/all_to_all | solution.py:303
  82.7 51.5 %copy-start = (bf16[2,256,1408]{2,1,0:T(8,128)(2,1)S(1)}, bf16[2,256,1408]{2,1,0:T(8,128)(2,1)}, u32[]{:S(2)}) copy-start(bf16[2,256,1408]{2,1,0:T(8,128)(2,1)} %cot_ref.5) | copy-start | bytes 4325380
  100.7 5.1 %collective-permute-start = (f32[1,1408]{1,0:T(1,128)S(1)}, f32[1,1408]{1,0:T(1,128)S(1)}, u32[]{:S(2)}, u32[]{:S(2)}) collective-permute-start(f32[1,1408]{1,0:T(1,128)S(1)} %psum.7), channel_id=1, source_target_pairs={{0,64},{16,80},{32,96},{48,112},{64,128},{80,144},{96,160},{112,17... | collective-permute-start | bytes 16904 | tf_op jit(solution)/shard_map/ppermute | solution.py:312
  102.1 4.0 %collective-permute-start.1 = (f32[1,1408]{1,0:T(1,128)S(1)}, f32[1,1408]{1,0:T(1,128)S(1)}, u32[]{:S(2)}, u32[]{:S(2)}) collective-permute-start(f32[1,1408]{1,0:T(1,128)S(1)} %psum.7), channel_id=1, source_target_pairs={{0,128},{16,144},{32,160},{48,176},{64,192},{80,208},{96,224},{112... | collective-permute-start | bytes 16904 | tf_op jit(solution)/shard_map/ppermute | solution.py:312
  104.6 2.8 %collective-permute-start.2 = (f32[1,1408]{1,0:T(1,128)S(1)}, f32[1,1408]{1,0:T(1,128)S(1)}, u32[]{:S(2)}, u32[]{:S(2)}) collective-permute-start(f32[1,1408]{1,0:T(1,128)S(1)} %psum.7), channel_id=1, source_target_pairs={{0,192},{16,208},{32,224},{48,240},{64,0},{80,16},{96,32},{112,48}... | collective-permute-start | bytes 16904 | tf_op jit(solution)/shard_map/ppermute | solution.py:312

commit v5 on v4

--- a/solution.py
+++ b/solution.py
@@ -45,20 +45,41 @@
     return even, odd
 
 
-def pack_kernel(low, high, x_ref, cot_ref, w_ref, out_ref):
+def pack_kernel(low, high, x_hbm, cot_hbm, w_hbm, out_hbm, x_ref, cot_ref, w_ref, out_ref, load_sems, store_sems):
     _, patches, d = x_ref.shape
-    homes = out_ref.shape[0] // (TILE * (high - low))
-
-    def rows(ref):
-        even, odd = to_quads(*[ref[f].astype(jnp.float32).reshape(patches // TILE, TILE, d) for f in range(2)])
-        per_home = patches // homes // TILE
+    total = out_ref.shape[0]
+    homes = total // (TILE * (high - low))
+    per_home = patches // homes // TILE
+    loads = [
+        pltpu.make_async_copy(source, target, load_sems.at[k])
+        for k, (source, target) in enumerate(((cot_hbm, cot_ref), (w_hbm, w_ref), (x_hbm, x_ref)))
+    ]
+    for load in loads:
+        load.start()
+
+    def rows(ref, part, parts):
+        size = patches // parts
+        block = [ref[f, part * size : (part + 1) * size].astype(jnp.float32) for f in range(2)]
+        even, odd = to_quads(*[values.reshape(size // TILE, TILE, d) for values in block])
         found = [
-            (even, odd)[q % 2][home * per_home + q // 2] for home in range(homes) for q in range(low, high)
+            (even, odd)[q % 2][home * per_home + q // 2] for home in range(homes // parts) for q in range(low, high)
         ]
         return jnp.concatenate(found, axis=0).astype(jnp.bfloat16)
 
-    out_ref[:, :d] = rows(x_ref)
-    out_ref[:, d:] = dot_nt(rows(cot_ref), w_ref[...]).astype(jnp.bfloat16)
+    loads[0].wait()
+    cot = rows(cot_ref, 0, 1)
+    loads[1].wait()
+    out_ref[:, d:] = dot_nt(cot, w_ref[...]).astype(jnp.bfloat16)
+    loads[2].wait()
+    half = total // 2
+    stores = []
+    for part in range(2):
+        at = pl.ds(part * half, half)
+        out_ref[at, :d] = rows(x_ref, part, 2)
+        stores.append(pltpu.make_async_copy(out_ref.at[at], out_hbm.at[at], store_sems.at[part]))
+        stores[part].start()
+    for store in stores:
+        store.wait()
 
 
 def late_kernel(quads, clip_ref, block, gain_ref, w_hbm, before_ref, *refs):
@@ -223,17 +244,22 @@
 
 
 def pack(low, high, frames, cotangent, w_out, members):
-    each, patches, d = frames.shape
-    inner = w_out.shape[0]
-    steps = 2
+    inner, d = w_out.shape
     rows = members * (high - low) * TILE
-    tokens = pl.BlockSpec((each, patches // steps, d), lambda i: (0, i, 0))
+    anywhere = pl.BlockSpec(memory_space=pl.ANY)
     return pl.pallas_call(
         functools.partial(pack_kernel, low, high),
-        grid=(steps,),
         out_shape=jax.ShapeDtypeStruct((rows, d + inner), jnp.bfloat16),
-        in_specs=[tokens, tokens, pl.BlockSpec((inner, d), lambda i: (0, 0))],
-        out_specs=pl.BlockSpec((rows // steps, d + inner), lambda i: (i, 0)),
+        in_specs=[anywhere] * 3,
+        out_specs=anywhere,
+        scratch_shapes=[
+            pltpu.VMEM(frames.shape, jnp.bfloat16),
+            pltpu.VMEM(cotangent.shape, jnp.bfloat16),
+            pltpu.VMEM(w_out.shape, jnp.bfloat16),
+            pltpu.VMEM((rows, d + inner), jnp.bfloat16),
+            pltpu.SemaphoreType.DMA((3,)),
+            pltpu.SemaphoreType.DMA((2,)),
+        ],
         compiler_params=params(WHOLE_VMEM_BYTES),
         cost_estimate=pl.CostEstimate(
             flops=2 * rows * d * inner, bytes_accessed=2 * (d * inner + 4 * rows * d), transcendentals=0

time: 136 us -> 136 us (level)
  no operation moved by 1% of the time
where the time goes in v5:
time: 136 us; the launch traced here: 135 us
  waiting for transfers between devices  44.5 us (33%)
  Pallas kernels  33.2 us (24%)
  blocking collectives  32.4 us (24%)
  starting transfers between devices  23.6 us (17%)
    all_to_all x3, waiting for transfers between devices, to_all(): return lax.all_to_all(block, 'ctx', 0, 0, tiled=True)  42.9 us
    pallas_call x2, Pallas kernels, attend(): pl.pallas_call(functools.partial(late_kernel if more else attend_kernel,...  23.4 us
    all_to_all x1, blocking collectives, to_all(): return lax.all_to_all(block, 'ctx', 0, 0, tiled=True)  22.8 us
    all_to_all x3, starting transfers between devices, to_all(): return lax.all_to_all(block, 'ctx', 0, 0, tiled=True)  18.7 us
    psum x1, blocking collectives, sum_groups(): value = lax.psum(value, 'dp', axis_index_groups=rows)  9.6 us
    pallas_call x2, Pallas kernels, pack(): pl.pallas_call(functools.partial(pack_kernel, low, high), out_shape=jax.S...  8.1 us
    ppermute x3, starting transfers between devices, sum_groups(): lax.ppermute(value, 'dp', [(i, (i + k * side) % groups) for i in range(gr...  4.9 us
  transfers between devices with their start and end apart: 6, of which 5 were waited for; matrix products, arithmetic and copies ran while one was open for 1% of the time, Pallas kernels for 20%

profile of v5, /device:TPU:1, one launch (start us, length us, event | category | flops | bytes accessed | tf_op | source)
XLA Modules:
  0.0 135.2 jit_solution(14349977022335516281)
XLA Ops:
  0.6 4.5 %pack_0.1 = bf16[384,2112]{1,0:T(8,128)(2,1)} custom-call(bf16[2,256,1408]{2,1,0:T(8,128)(2,1)} %x_hbm.3, bf16[2,256,1408]{2,1,0:T(8,128)(2,1)} %cot_ref.1, bf16[704,1408]{1,0:T(8,128)(2,1)} %w_hbm.3), custom_call_target="tpu_custom_call" | custom-call | flops 761266176 | bytes 6307840 | tf_op jit(solution)/shard_map/pack_0/pallas_call | solution.py:250
  5.1 10.0 %all-to-all-start = ((bf16[16,24,2112]{2,1,0:T(8,128)(2,1)}), bf16[16,24,2112]{2,1,0:T(8,128)(2,1)S(1)}, u32[]{:S(2)}, u32[]{:S(2)}) async-start(bf16[16,24,2112]{2,1,0:T(8,128)(2,1)} %bitcast.20), calls=%async_computation | async-start | bytes 3342336 | tf_op jit(solution)/shard_map/all_to_all | solution.py:329
  15.1 3.6 %pack_3.1 = bf16[128,2112]{1,0:T(8,128)(2,1)} custom-call(bf16[2,256,1408]{2,1,0:T(8,128)(2,1)} %x_hbm.3, bf16[2,256,1408]{2,1,0:T(8,128)(2,1)} %cot_ref.1, bf16[704,1408]{1,0:T(8,128)(2,1)} %w_hbm.3), custom_call_target="tpu_custom_call" | custom-call | flops 253755392 | bytes 3424256 | tf_op jit(solution)/shard_map/pack_3/pallas_call | solution.py:250
  18.7 36.8 %all-to-all-done = bf16[16,24,2112]{2,1,0:T(8,128)(2,1)S(1)} async-done(((bf16[16,24,2112]{2,1,0:T(8,128)(2,1)}), bf16[16,24,2112]{2,1,0:T(8,128)(2,1)S(1)}, u32[]{:S(2)}, u32[]{:S(2)}) %all-to-all-start) | async-done | bytes 1622048 | tf_op jit(solution)/shard_map/all_to_all | solution.py:329
  55.5 0.0 copy-start.1
  55.5 4.4 %all-to-all-start.2 = ((bf16[16,8,2112]{2,1,0:T(8,128)(2,1)}), bf16[16,8,2112]{2,1,0:T(8,128)(2,1)S(1)}, u32[]{:S(2)}, u32[]{:S(2)}) async-start(bf16[16,8,2112]{2,1,0:T(8,128)(2,1)} %bitcast.22), calls=%async_computation.2 | async-start | bytes 1114112 | tf_op jit(solution)/shard_map/all_to_all | solution.py:329
  59.9 0.0 copy-done.1
  59.9 15.0 %attend_3.1 = (bf16[384,1408]{1,0:T(8,128)(2,1)}, f32[1,1408]{1,0:T(1,128)}) custom-call(s32[1,32]{1,0:T(1,128)} %clip_ref.3, bf16[384,2112]{1,0:T(8,128)(2,1)} %bitcast.19, f32[1408]{0:T(1024)} %gain_ref.3, bf16[2112,1408]{1,0:T(8,128)(2,1)} %bitcast.17), custom_call_target="tpu_custom_call" | custom-call | tf_op jit(solution)/shard_map/attend_3/pallas_call | solution.py:279
  74.9 2.9 %all-to-all-done.2 = bf16[16,8,2112]{2,1,0:T(8,128)(2,1)S(1)} async-done(((bf16[16,8,2112]{2,1,0:T(8,128)(2,1)}), bf16[16,8,2112]{2,1,0:T(8,128)(2,1)S(1)}, u32[]{:S(2)}, u32[]{:S(2)}) %all-to-all-start.2) | async-done | bytes 540704 | tf_op jit(solution)/shard_map/all_to_all | solution.py:329
  77.9 0.0 copy-start.2
  77.9 4.3 %all-to-all-start.1 = ((bf16[16,24,1408]{2,1,0:T(8,128)(2,1)}), bf16[16,24,1408]{2,1,0:T(8,128)(2,1)S(1)}, u32[]{:S(2)}, u32[]{:S(2)}) async-start(bf16[16,24,1408]{2,1,0:T(8,128)(2,1)} %bitcast.23), calls=%async_computation.1 | async-start | bytes 2162688 | tf_op jit(solution)/shard_map/all_to_all | solution.py:329
  82.2 0.0 copy-done.2
  82.2 0.0 copy-start
  82.2 8.4 %attend_1.1 = (bf16[128,1792]{1,0:T(8,128)(2,1)}, f32[1,1408]{1,0:T(1,128)}) custom-call(s32[1,32]{1,0:T(1,128)} %clip_ref.3, bf16[128,2112]{1,0:T(8,128)(2,1)} %bitcast.21, f32[1408]{0:T(1024)} %gain_ref.3, bf16[2112,1408]{1,0:T(8,128)(2,1)} %bitcast.18, f32[1,1408]{1,0:T(1,128)} %get-tuple-element.13.before_ref), custom_call_target="tpu_custom_call" | custom-call | tf_op jit(solution)/shard_map/attend_1/pallas_call | solution.py:279
  90.6 9.6 %psum.7 = f32[1,1408]{1,0:T(1,128)S(1)} all-reduce(f32[1,1408]{1,0:T(1,128)} %get-tuple-element.15), channel_id=1, replica_groups={{0,16,32,48},{64,80,96,112},{128,144,160,176},{192,208,224,240},{1,17,3..., use_global_device_ids=true, to_apply=%region_0.0 | all-reduce | flops 1408 | bytes 11264 | tf_op jit(solution)/shard_map/psum | solution.py:337
  100.2 1.3 collective-permute-start
  101.5 2.5 %collective-permute-start.1 = (f32[1,1408]{1,0:T(1,128)S(1)}, f32[1,1408]{1,0:T(1,128)S(1)}, u32[]{:S(2)}, u32[]{:S(2)}) collective-permute-start(f32[1,1408]{1,0:T(1,128)S(1)} %psum.7), channel_id=1, source_target_pairs={{0,128},{16,144},{32,160},{48,176},{64,192},{80,208},{96,224},{112... | collective-permute-start | bytes 16904 | tf_op jit(solution)/shard_map/ppermute | solution.py:338
  104.0 1.2 collective-permute-start.2
  105.1 0.0 collective-permute-done
  105.1 0.3 collective-permute-done.1
  105.5 1.3 collective-permute-done.2
  106.9 0.7 bitcast_dynamic-update-slice_fusion
  107.5 3.2 %all-to-all-done.1 = bf16[16,24,1408]{2,1,0:T(8,128)(2,1)S(1)} async-done(((bf16[16,24,1408]{2,1,0:T(8,128)(2,1)}), bf16[16,24,1408]{2,1,0:T(8,128)(2,1)S(1)}, u32[]{:S(2)}, u32[]{:S(2)}) %all-to-all-start.1) | async-done | bytes 1081376 | tf_op jit(solution)/shard_map/all_to_all | solution.py:329
  110.8 22.8 %all_to_all.46 = bf16[16,8,1792]{2,1,0:T(8,128)(2,1)S(1)} all-to-all(bf16[16,8,1792]{2,1,0:T(8,128)(2,1)} %bitcast.24), channel_id=1, replica_groups=mesh['dp'=16,'ctx'=16] {'ctx'}, dimensions={0} | all-to-all | bytes 917504 | tf_op jit(solution)/shard_map/all_to_all | solution.py:329
  133.5 0.0 copy-done
  133.5 1.7 %finish.1 = (bf16[2,256,1408]{2,1,0:T(8,128)(2,1)}, f32[1408]{0:T(1024)}) custom-call(bf16[2,256,1408]{2,1,0:T(8,128)(2,1)S(1)} %copy-done, bf16[384,1408]{1,0:T(8,128)(2,1)S(1)} %bitcast.15, bf16[128,1792]{1,0:T(8,128)(2,1)S(1)} %bitcast.16), custom_call_target="tpu_custom_call" | custom-call | tf_op jit(solution)/shard_map/finish/pallas_call | solution.py:303
  (8 shorter events, 0.1 us)
Async XLA Ops:
  5.1 50.4 %all-to-all-start = ((bf16[16,24,2112]{2,1,0:T(8,128)(2,1)}), bf16[16,24,2112]{2,1,0:T(8,128)(2,1)S(1)}, u32[]{:S(2)}, u32[]{:S(2)}) async-start(bf16[16,24,2112]{2,1,0:T(8,128)(2,1)} %bitcast.20), calls=%async_computation | async-start | bytes 3342336 | tf_op jit(solution)/shard_map/all_to_all | solution.py:329
  55.5 4.4 %copy-start.1 = (bf16[16,24,2112]{2,1,0:T(8,128)(2,1)}, bf16[16,24,2112]{2,1,0:T(8,128)(2,1)S(1)}, u32[]{:S(2)}) copy-start(bf16[16,24,2112]{2,1,0:T(8,128)(2,1)S(1)} %all-to-all-done) | copy-start | bytes 4866052
  55.5 22.4 %all-to-all-start.2 = ((bf16[16,8,2112]{2,1,0:T(8,128)(2,1)}), bf16[16,8,2112]{2,1,0:T(8,128)(2,1)S(1)}, u32[]{:S(2)}, u32[]{:S(2)}) async-start(bf16[16,8,2112]{2,1,0:T(8,128)(2,1)} %bitcast.22), calls=%async_computation.2 | async-start | bytes 1114112 | tf_op jit(solution)/shard_map/all_to_all | solution.py:329
  77.9 4.3 %copy-start.2 = (bf16[16,8,2112]{2,1,0:T(8,128)(2,1)}, bf16[16,8,2112]{2,1,0:T(8,128)(2,1)S(1)}, u32[]{:S(2)}) copy-start(bf16[16,8,2112]{2,1,0:T(8,128)(2,1)S(1)} %all-to-all-done.2) | copy-start | bytes 1622020
  77.9 32.9 %all-to-all-start.1 = ((bf16[16,24,1408]{2,1,0:T(8,128)(2,1)}), bf16[16,24,1408]{2,1,0:T(8,128)(2,1)S(1)}, u32[]{:S(2)}, u32[]{:S(2)}) async-start(bf16[16,24,1408]{2,1,0:T(8,128)(2,1)} %bitcast.23), calls=%async_computation.1 | async-start | bytes 2162688 | tf_op jit(solution)/shard_map/all_to_all | solution.py:329
  82.2 51.4 %copy-start = (bf16[2,256,1408]{2,1,0:T(8,128)(2,1)S(1)}, bf16[2,256,1408]{2,1,0:T(8,128)(2,1)}, u32[]{:S(2)}) copy-start(bf16[2,256,1408]{2,1,0:T(8,128)(2,1)} %cot_ref.1) | copy-start | bytes 4325380
  100.2 4.9 %collective-permute-start = (f32[1,1408]{1,0:T(1,128)S(1)}, f32[1,1408]{1,0:T(1,128)S(1)}, u32[]{:S(2)}, u32[]{:S(2)}) collective-permute-start(f32[1,1408]{1,0:T(1,128)S(1)} %psum.7), channel_id=1, source_target_pairs={{0,64},{16,80},{32,96},{48,112},{64,128},{80,144},{96,160},{112,17... | collective-permute-start | bytes 16904 | tf_op jit(solution)/shard_map/ppermute | solution.py:338
  101.5 4.0 %collective-permute-start.1 = (f32[1,1408]{1,0:T(1,128)S(1)}, f32[1,1408]{1,0:T(1,128)S(1)}, u32[]{:S(2)}, u32[]{:S(2)}) collective-permute-start(f32[1,1408]{1,0:T(1,128)S(1)} %psum.7), channel_id=1, source_target_pairs={{0,128},{16,144},{32,160},{48,176},{64,192},{80,208},{96,224},{112... | collective-permute-start | bytes 16904 | tf_op jit(solution)/shard_map/ppermute | solution.py:338
  104.0 2.8 %collective-permute-start.2 = (f32[1,1408]{1,0:T(1,128)S(1)}, f32[1,1408]{1,0:T(1,128)S(1)}, u32[]{:S(2)}, u32[]{:S(2)}) collective-permute-start(f32[1,1408]{1,0:T(1,128)S(1)} %psum.7), channel_id=1, source_target_pairs={{0,192},{16,208},{32,224},{48,240},{64,0},{80,16},{96,32},{112,48}... | collective-permute-start | bytes 16904 | tf_op jit(solution)/shard_map/ppermute | solution.py:338

commit v6 on v5

--- a/solution.py
+++ b/solution.py
@@ -206,33 +206,35 @@
     lax.fori_loop(0, sources // step, back_step, 0)
 
 
-def finish_kernel(cot_ref, early_ref, late_ref, out_ref, sum_ref, rider):
+def finish_kernel(cot_ref, early_ref, late_ref, out_hbm, sum_ref, out_ref, sems):
     _, patches, d = cot_ref.shape
-    late_rows = late_ref.shape[0]
-    homes = late_rows // TILE
-    early = early_ref[...].astype(jnp.float32).reshape(homes, -1, d)
-    late = late_ref[...].astype(jnp.float32).reshape(homes, TILE, -1)
-    term = jnp.concatenate([early, late[:, :, :d]], axis=1).reshape(patches // TILE, 2 * TILE, d)
-    terms = to_quads(term[:, :TILE], term[:, TILE:])
-    for f in range(2):
-        total = cot_ref[f].astype(jnp.float32) + terms[f].reshape(patches, d)
-        out_ref[f] = total.astype(jnp.bfloat16)
-
-    @pl.when(pl.program_id(0) == 0)
-    def _():
-        rider[...] = jnp.zeros_like(rider)
-
-    rider[...] += jnp.sum(late[:, :, d:], axis=0)
-
-    @pl.when(pl.program_id(0) == pl.num_programs(0) - 1)
-    def _():
-        over = d // 128 - TILE
-        for row in range(d // 128):
-            if row < TILE:
-                both = rider[row, :128] + rider[row, 256:]
-            else:
-                both = rider[row - TILE, 128:256] + rider[row - TILE + over, 128:256]
-            sum_ref[row * 128 : (row + 1) * 128] = both
+    parts = sems.shape[0]
+    homes = late_ref.shape[0] // TILE
+    few, size = homes // parts, patches // parts
+    rider = jnp.zeros((TILE, late_ref.shape[1] - d), jnp.float32)
+    stores = []
+    for part in range(parts):
+        many = early_ref.shape[0] // parts
+        early = early_ref[part * many : (part + 1) * many].astype(jnp.float32).reshape(few, -1, d)
+        late = late_ref[part * few * TILE : (part + 1) * few * TILE].astype(jnp.float32).reshape(few, TILE, -1)
+        term = jnp.concatenate([early, late[:, :, :d]], axis=1).reshape(size // TILE, 2 * TILE, d)
+        terms = to_quads(term[:, :TILE], term[:, TILE:])
+        for f in range(2):
+            total = cot_ref[f, part * size : (part + 1) * size].astype(jnp.float32) + terms[f].reshape(size, d)
+            out_ref[f, part * size : (part + 1) * size] = total.astype(jnp.bfloat16)
+        at = pl.ds(part * size, size)
+        stores.append(pltpu.make_async_copy(out_ref.at[:, at], out_hbm.at[:, at], sems.at[part]))
+        stores[part].start()
+        rider = rider + jnp.sum(late[:, :, d:], axis=0)
+    over = d // 128 - TILE
+    for row in range(d // 128):
+        if row < TILE:
+            both = rider[row, :128] + rider[row, 256:]
+        else:
+            both = rider[row - TILE, 128:256] + rider[row - TILE + over, 128:256]
+        sum_ref[row * 128 : (row + 1) * 128] = both
+    for store in stores:
+        store.wait()
 
 
 def vmem(count):
@@ -296,21 +298,17 @@
 
 
 def finish(cotangent, early, late):
-    each, patches, d = cotangent.shape
-    steps = 2
-    tokens = pl.BlockSpec((each, patches // steps, d), lambda i: (0, i, 0))
-    extra = late.shape[1] - d
+    d = cotangent.shape[2]
+    parts = 4
     return pl.pallas_call(
         finish_kernel,
-        grid=(steps,),
         out_shape=(
             jax.ShapeDtypeStruct(cotangent.shape, jnp.bfloat16),
             jax.ShapeDtypeStruct((d,), jnp.float32),
         ),
-        in_specs=[tokens]
-        + [pl.BlockSpec((rows.shape[0] // steps, rows.shape[1]), lambda i: (i, 0)) for rows in (early, late)],
-        out_specs=(tokens, pl.BlockSpec((d,), lambda i: (0,))),
-        scratch_shapes=[pltpu.VMEM((TILE, extra), jnp.float32)],
+        in_specs=vmem(3),
+        out_specs=(pl.BlockSpec(memory_space=pl.ANY), vmem(1)[0]),
+        scratch_shapes=[pltpu.VMEM(cotangent.shape, jnp.bfloat16), pltpu.SemaphoreType.DMA((parts,))],
         compiler_params=params(VMEM_BYTES),
         name="finish",
     )(cotangent, early, late)

time: 136 us -> 136 us (level)
  no operation moved by 1% of the time
where the time goes in v6:
time: 136 us
  waiting for transfers between devices  44.5 us (33%)
  Pallas kernels  33.5 us (25%)
  blocking collectives  32.4 us (24%)
  starting transfers between devices  23.6 us (17%)
    all_to_all x3, waiting for transfers between devices, to_all(): return lax.all_to_all(block, 'ctx', 0, 0, tiled=True)  42.9 us
    pallas_call x2, Pallas kernels, attend(): pl.pallas_call(functools.partial(late_kernel if more else attend_kernel,...  23.4 us
    all_to_all x1, blocking collectives, to_all(): return lax.all_to_all(block, 'ctx', 0, 0, tiled=True)  22.8 us
    all_to_all x3, starting transfers between devices, to_all(): return lax.all_to_all(block, 'ctx', 0, 0, tiled=True)  18.7 us
    psum x1, blocking collectives, sum_groups(): value = lax.psum(value, 'dp', axis_index_groups=rows)  9.6 us
    pallas_call x2, Pallas kernels, pack(): pl.pallas_call(functools.partial(pack_kernel, low, high), out_shape=jax.S...  8.1 us
    ppermute x3, starting transfers between devices, sum_groups(): lax.ppermute(value, 'dp', [(i, (i + k * side) % groups) for i in range(gr...  4.9 us
  transfers between devices with their start and end apart: 6, of which 5 were waited for; matrix products, arithmetic and copies ran while one was open for 1% of the time, Pallas kernels for 20%

profile of v6, /device:TPU:1, one launch (start us, length us, event | category | flops | bytes accessed | tf_op | source)
XLA Modules:
  0.0 135.7 jit_solution(17371826706491101301)
XLA Ops:
  0.6 4.5 %pack_0.1 = bf16[384,2112]{1,0:T(8,128)(2,1)} custom-call(bf16[2,256,1408]{2,1,0:T(8,128)(2,1)} %x_hbm.3, bf16[2,256,1408]{2,1,0:T(8,128)(2,1)} %cot_ref.1, bf16[704,1408]{1,0:T(8,128)(2,1)} %w_hbm.3), custom_call_target="tpu_custom_call" | custom-call | flops 761266176 | bytes 6307840 | tf_op jit(solution)/shard_map/pack_0/pallas_call | solution.py:252
  5.1 10.0 %all-to-all-start = ((bf16[16,24,2112]{2,1,0:T(8,128)(2,1)}), bf16[16,24,2112]{2,1,0:T(8,128)(2,1)S(1)}, u32[]{:S(2)}, u32[]{:S(2)}) async-start(bf16[16,24,2112]{2,1,0:T(8,128)(2,1)} %bitcast.20), calls=%async_computation | async-start | bytes 3342336 | tf_op jit(solution)/shard_map/all_to_all | solution.py:327
  15.1 3.6 %pack_3.1 = bf16[128,2112]{1,0:T(8,128)(2,1)} custom-call(bf16[2,256,1408]{2,1,0:T(8,128)(2,1)} %x_hbm.3, bf16[2,256,1408]{2,1,0:T(8,128)(2,1)} %cot_ref.1, bf16[704,1408]{1,0:T(8,128)(2,1)} %w_hbm.3), custom_call_target="tpu_custom_call" | custom-call | flops 253755392 | bytes 3424256 | tf_op jit(solution)/shard_map/pack_3/pallas_call | solution.py:252
  18.7 36.8 %all-to-all-done = bf16[16,24,2112]{2,1,0:T(8,128)(2,1)S(1)} async-done(((bf16[16,24,2112]{2,1,0:T(8,128)(2,1)}), bf16[16,24,2112]{2,1,0:T(8,128)(2,1)S(1)}, u32[]{:S(2)}, u32[]{:S(2)}) %all-to-all-start) | async-done | bytes 1622048 | tf_op jit(solution)/shard_map/all_to_all | solution.py:327
  55.5 0.0 copy-start.1
  55.5 4.4 %all-to-all-start.2 = ((bf16[16,8,2112]{2,1,0:T(8,128)(2,1)}), bf16[16,8,2112]{2,1,0:T(8,128)(2,1)S(1)}, u32[]{:S(2)}, u32[]{:S(2)}) async-start(bf16[16,8,2112]{2,1,0:T(8,128)(2,1)} %bitcast.22), calls=%async_computation.2 | async-start | bytes 1114112 | tf_op jit(solution)/shard_map/all_to_all | solution.py:327
  59.9 0.0 copy-done.1
  59.9 15.0 %attend_3.1 = (bf16[384,1408]{1,0:T(8,128)(2,1)}, f32[1,1408]{1,0:T(1,128)}) custom-call(s32[1,32]{1,0:T(1,128)} %clip_ref.3, bf16[384,2112]{1,0:T(8,128)(2,1)} %bitcast.19, f32[1408]{0:T(1024)} %gain_ref.3, bf16[2112,1408]{1,0:T(8,128)(2,1)} %bitcast.17), custom_call_target="tpu_custom_call" | custom-call | tf_op jit(solution)/shard_map/attend_3/pallas_call | solution.py:281
  74.9 2.9 %all-to-all-done.2 = bf16[16,8,2112]{2,1,0:T(8,128)(2,1)S(1)} async-done(((bf16[16,8,2112]{2,1,0:T(8,128)(2,1)}), bf16[16,8,2112]{2,1,0:T(8,128)(2,1)S(1)}, u32[]{:S(2)}, u32[]{:S(2)}) %all-to-all-start.2) | async-done | bytes 540704 | tf_op jit(solution)/shard_map/all_to_all | solution.py:327
  77.9 0.0 copy-start.2
  77.9 4.3 %all-to-all-start.1 = ((bf16[16,24,1408]{2,1,0:T(8,128)(2,1)}), bf16[16,24,1408]{2,1,0:T(8,128)(2,1)S(1)}, u32[]{:S(2)}, u32[]{:S(2)}) async-start(bf16[16,24,1408]{2,1,0:T(8,128)(2,1)} %bitcast.23), calls=%async_computation.1 | async-start | bytes 2162688 | tf_op jit(solution)/shard_map/all_to_all | solution.py:327
  82.2 0.0 copy-done.2
  82.2 0.0 copy-start
  82.2 8.4 %attend_1.1 = (bf16[128,1792]{1,0:T(8,128)(2,1)}, f32[1,1408]{1,0:T(1,128)}) custom-call(s32[1,32]{1,0:T(1,128)} %clip_ref.3, bf16[128,2112]{1,0:T(8,128)(2,1)} %bitcast.21, f32[1408]{0:T(1024)} %gain_ref.3, bf16[2112,1408]{1,0:T(8,128)(2,1)} %bitcast.18, f32[1,1408]{1,0:T(1,128)} %get-tuple-element.13.before_ref), custom_call_target="tpu_custom_call" | custom-call | tf_op jit(solution)/shard_map/attend_1/pallas_call | solution.py:281
  90.6 9.6 %psum.7 = f32[1,1408]{1,0:T(1,128)S(1)} all-reduce(f32[1,1408]{1,0:T(1,128)} %get-tuple-element.15), channel_id=1, replica_groups={{0,16,32,48},{64,80,96,112},{128,144,160,176},{192,208,224,240},{1,17,3..., use_global_device_ids=true, to_apply=%region_0.0 | all-reduce | flops 1408 | bytes 11264 | tf_op jit(solution)/shard_map/psum | solution.py:335
  100.2 1.3 collective-permute-start
  101.5 2.5 %collective-permute-start.1 = (f32[1,1408]{1,0:T(1,128)S(1)}, f32[1,1408]{1,0:T(1,128)S(1)}, u32[]{:S(2)}, u32[]{:S(2)}) collective-permute-start(f32[1,1408]{1,0:T(1,128)S(1)} %psum.7), channel_id=1, source_target_pairs={{0,128},{16,144},{32,160},{48,176},{64,192},{80,208},{96,224},{112... | collective-permute-start | bytes 16904 | tf_op jit(solution)/shard_map/ppermute | solution.py:336
  104.0 1.2 collective-permute-start.2
  105.1 0.0 collective-permute-done
  105.1 0.3 collective-permute-done.1
  105.5 1.3 collective-permute-done.2
  106.9 0.7 bitcast_dynamic-update-slice_fusion
  107.5 3.2 %all-to-all-done.1 = bf16[16,24,1408]{2,1,0:T(8,128)(2,1)S(1)} async-done(((bf16[16,24,1408]{2,1,0:T(8,128)(2,1)}), bf16[16,24,1408]{2,1,0:T(8,128)(2,1)S(1)}, u32[]{:S(2)}, u32[]{:S(2)}) %all-to-all-start.1) | async-done | bytes 1081376 | tf_op jit(solution)/shard_map/all_to_all | solution.py:327
  110.8 22.8 %all_to_all.46 = bf16[16,8,1792]{2,1,0:T(8,128)(2,1)S(1)} all-to-all(bf16[16,8,1792]{2,1,0:T(8,128)(2,1)} %bitcast.24), channel_id=1, replica_groups=mesh['dp'=16,'ctx'=16] {'ctx'}, dimensions={0} | all-to-all | bytes 917504 | tf_op jit(solution)/shard_map/all_to_all | solution.py:327
  133.5 0.0 copy-done
  133.5 2.0 %finish.1 = (bf16[2,256,1408]{2,1,0:T(8,128)(2,1)}, f32[1408]{0:T(1024)}) custom-call(bf16[2,256,1408]{2,1,0:T(8,128)(2,1)S(1)} %copy-done, bf16[384,1408]{1,0:T(8,128)(2,1)S(1)} %bitcast.15, bf16[128,1792]{1,0:T(8,128)(2,1)S(1)} %bitcast.16), custom_call_target="tpu_custom_call" | custom-call | tf_op jit(solution)/shard_map/finish/pallas_call | solution.py:303
  (8 shorter events, 0.1 us)
Async XLA Ops:
  5.1 50.4 %all-to-all-start = ((bf16[16,24,2112]{2,1,0:T(8,128)(2,1)}), bf16[16,24,2112]{2,1,0:T(8,128)(2,1)S(1)}, u32[]{:S(2)}, u32[]{:S(2)}) async-start(bf16[16,24,2112]{2,1,0:T(8,128)(2,1)} %bitcast.20), calls=%async_computation | async-start | bytes 3342336 | tf_op jit(solution)/shard_map/all_to_all | solution.py:327
  55.5 4.4 %copy-start.1 = (bf16[16,24,2112]{2,1,0:T(8,128)(2,1)}, bf16[16,24,2112]{2,1,0:T(8,128)(2,1)S(1)}, u32[]{:S(2)}) copy-start(bf16[16,24,2112]{2,1,0:T(8,128)(2,1)S(1)} %all-to-all-done) | copy-start | bytes 4866052
  55.5 22.4 %all-to-all-start.2 = ((bf16[16,8,2112]{2,1,0:T(8,128)(2,1)}), bf16[16,8,2112]{2,1,0:T(8,128)(2,1)S(1)}, u32[]{:S(2)}, u32[]{:S(2)}) async-start(bf16[16,8,2112]{2,1,0:T(8,128)(2,1)} %bitcast.22), calls=%async_computation.2 | async-start | bytes 1114112 | tf_op jit(solution)/shard_map/all_to_all | solution.py:327
  77.9 4.3 %copy-start.2 = (bf16[16,8,2112]{2,1,0:T(8,128)(2,1)}, bf16[16,8,2112]{2,1,0:T(8,128)(2,1)S(1)}, u32[]{:S(2)}) copy-start(bf16[16,8,2112]{2,1,0:T(8,128)(2,1)S(1)} %all-to-all-done.2) | copy-start | bytes 1622020
  77.9 32.9 %all-to-all-start.1 = ((bf16[16,24,1408]{2,1,0:T(8,128)(2,1)}), bf16[16,24,1408]{2,1,0:T(8,128)(2,1)S(1)}, u32[]{:S(2)}, u32[]{:S(2)}) async-start(bf16[16,24,1408]{2,1,0:T(8,128)(2,1)} %bitcast.23), calls=%async_computation.1 | async-start | bytes 2162688 | tf_op jit(solution)/shard_map/all_to_all | solution.py:327
  82.2 51.4 %copy-start = (bf16[2,256,1408]{2,1,0:T(8,128)(2,1)S(1)}, bf16[2,256,1408]{2,1,0:T(8,128)(2,1)}, u32[]{:S(2)}) copy-start(bf16[2,256,1408]{2,1,0:T(8,128)(2,1)} %cot_ref.1) | copy-start | bytes 4325380
  100.2 4.9 %collective-permute-start = (f32[1,1408]{1,0:T(1,128)S(1)}, f32[1,1408]{1,0:T(1,128)S(1)}, u32[]{:S(2)}, u32[]{:S(2)}) collective-permute-start(f32[1,1408]{1,0:T(1,128)S(1)} %psum.7), channel_id=1, source_target_pairs={{0,64},{16,80},{32,96},{48,112},{64,128},{80,144},{96,160},{112,17... | collective-permute-start | bytes 16904 | tf_op jit(solution)/shard_map/ppermute | solution.py:336
  101.5 4.0 %collective-permute-start.1 = (f32[1,1408]{1,0:T(1,128)S(1)}, f32[1,1408]{1,0:T(1,128)S(1)}, u32[]{:S(2)}, u32[]{:S(2)}) collective-permute-start(f32[1,1408]{1,0:T(1,128)S(1)} %psum.7), channel_id=1, source_target_pairs={{0,128},{16,144},{32,160},{48,176},{64,192},{80,208},{96,224},{112... | collective-permute-start | bytes 16904 | tf_op jit(solution)/shard_map/ppermute | solution.py:336
  104.0 2.8 %collective-permute-start.2 = (f32[1,1408]{1,0:T(1,128)S(1)}, f32[1,1408]{1,0:T(1,128)S(1)}, u32[]{:S(2)}, u32[]{:S(2)}) collective-permute-start(f32[1,1408]{1,0:T(1,128)S(1)} %psum.7), channel_id=1, source_target_pairs={{0,192},{16,208},{32,224},{48,240},{64,0},{80,16},{96,32},{112,48}... | collective-permute-start | bytes 16904 | tf_op jit(solution)/shard_map/ppermute | solution.py:336

commit v7 on v5

--- a/solution.py
+++ b/solution.py
@@ -12,7 +12,7 @@
 CLIPS = 3
 QUAD = 4
 TILE = 8
-PIECES = 4
+PIECES = 1
 RIDER = 384
 EARLY = 3
 VMEM_BYTES = 16 * 1024 * 1024

time: 136 us -> 136 us (level)
  no operation moved by 1% of the time
where the time goes in v7:
time: 136 us; the launch traced here: 135 us
  waiting for transfers between devices  44.6 us (33%)
  Pallas kernels  33.2 us (24%)
  blocking collectives  32.3 us (24%)
  starting transfers between devices  23.6 us (17%)
    all_to_all x3, waiting for transfers between devices, to_all(): return lax.all_to_all(block, 'ctx', 0, 0, tiled=True)  43 us
    pallas_call x2, Pallas kernels, attend(): pl.pallas_call(functools.partial(late_kernel if more else attend_kernel,...  23.4 us
    all_to_all x1, blocking collectives, to_all(): return lax.all_to_all(block, 'ctx', 0, 0, tiled=True)  22.7 us
    all_to_all x3, starting transfers between devices, to_all(): return lax.all_to_all(block, 'ctx', 0, 0, tiled=True)  18.7 us
    psum x1, blocking collectives, sum_groups(): value = lax.psum(value, 'dp', axis_index_groups=rows)  9.55 us
    pallas_call x2, Pallas kernels, pack(): pl.pallas_call(functools.partial(pack_kernel, low, high), out_shape=jax.S...  8.1 us
    ppermute x3, starting transfers between devices, sum_groups(): lax.ppermute(value, 'dp', [(i, (i + k * side) % groups) for i in range(gr...  4.9 us
  transfers between devices with their start and end apart: 6, of which 5 were waited for; matrix products, arithmetic and copies ran while one was open for 1% of the time, Pallas kernels for 20%

profile of v7, /device:TPU:1, one launch (start us, length us, event | category | flops | bytes accessed | tf_op | source)
XLA Modules:
  0.0 135.2 jit_solution(5564519730084837405)
XLA Ops:
  0.6 4.5 %pack_0.1 = bf16[384,2112]{1,0:T(8,128)(2,1)} custom-call(bf16[2,256,1408]{2,1,0:T(8,128)(2,1)} %x_hbm.3, bf16[2,256,1408]{2,1,0:T(8,128)(2,1)} %cot_ref.1, bf16[704,1408]{1,0:T(8,128)(2,1)} %w_hbm.3), custom_call_target="tpu_custom_call" | custom-call | flops 761266176 | bytes 6307840 | tf_op jit(solution)/shard_map/pack_0/pallas_call | solution.py:250
  5.1 10.0 %all-to-all-start = ((bf16[16,24,2112]{2,1,0:T(8,128)(2,1)}), bf16[16,24,2112]{2,1,0:T(8,128)(2,1)S(1)}, u32[]{:S(2)}, u32[]{:S(2)}) async-start(bf16[16,24,2112]{2,1,0:T(8,128)(2,1)} %bitcast.20), calls=%async_computation | async-start | bytes 3342336 | tf_op jit(solution)/shard_map/all_to_all | solution.py:329
  15.1 3.6 %pack_3.1 = bf16[128,2112]{1,0:T(8,128)(2,1)} custom-call(bf16[2,256,1408]{2,1,0:T(8,128)(2,1)} %x_hbm.3, bf16[2,256,1408]{2,1,0:T(8,128)(2,1)} %cot_ref.1, bf16[704,1408]{1,0:T(8,128)(2,1)} %w_hbm.3), custom_call_target="tpu_custom_call" | custom-call | flops 253755392 | bytes 3424256 | tf_op jit(solution)/shard_map/pack_3/pallas_call | solution.py:250
  18.7 36.8 %all-to-all-done = bf16[16,24,2112]{2,1,0:T(8,128)(2,1)S(1)} async-done(((bf16[16,24,2112]{2,1,0:T(8,128)(2,1)}), bf16[16,24,2112]{2,1,0:T(8,128)(2,1)S(1)}, u32[]{:S(2)}, u32[]{:S(2)}) %all-to-all-start) | async-done | bytes 1622048 | tf_op jit(solution)/shard_map/all_to_all | solution.py:329
  55.5 0.0 copy-start.1
  55.5 4.4 %all-to-all-start.2 = ((bf16[16,8,2112]{2,1,0:T(8,128)(2,1)}), bf16[16,8,2112]{2,1,0:T(8,128)(2,1)S(1)}, u32[]{:S(2)}, u32[]{:S(2)}) async-start(bf16[16,8,2112]{2,1,0:T(8,128)(2,1)} %bitcast.22), calls=%async_computation.2 | async-start | bytes 1114112 | tf_op jit(solution)/shard_map/all_to_all | solution.py:329
  59.9 0.0 copy-done.1
  59.9 15.0 %attend_3.1 = (bf16[384,1408]{1,0:T(8,128)(2,1)}, f32[1,1408]{1,0:T(1,128)}) custom-call(s32[1,32]{1,0:T(1,128)} %clip_ref.3, bf16[384,2112]{1,0:T(8,128)(2,1)} %bitcast.19, f32[1408]{0:T(1024)} %gain_ref.3, bf16[2112,1408]{1,0:T(8,128)(2,1)} %bitcast.17), custom_call_target="tpu_custom_call" | custom-call | tf_op jit(solution)/shard_map/attend_3/pallas_call | solution.py:279
  74.9 3.0 %all-to-all-done.2 = bf16[16,8,2112]{2,1,0:T(8,128)(2,1)S(1)} async-done(((bf16[16,8,2112]{2,1,0:T(8,128)(2,1)}), bf16[16,8,2112]{2,1,0:T(8,128)(2,1)S(1)}, u32[]{:S(2)}, u32[]{:S(2)}) %all-to-all-start.2) | async-done | bytes 540704 | tf_op jit(solution)/shard_map/all_to_all | solution.py:329
  77.9 0.0 copy-start.2
  77.9 4.3 %all-to-all-start.1 = ((bf16[16,24,1408]{2,1,0:T(8,128)(2,1)}), bf16[16,24,1408]{2,1,0:T(8,128)(2,1)S(1)}, u32[]{:S(2)}, u32[]{:S(2)}) async-start(bf16[16,24,1408]{2,1,0:T(8,128)(2,1)} %bitcast.23), calls=%async_computation.1 | async-start | bytes 2162688 | tf_op jit(solution)/shard_map/all_to_all | solution.py:329
  82.2 0.0 copy-done.2
  82.2 0.0 copy-start
  82.2 8.4 %attend_1.1 = (bf16[128,1792]{1,0:T(8,128)(2,1)}, f32[1,1408]{1,0:T(1,128)}) custom-call(s32[1,32]{1,0:T(1,128)} %clip_ref.3, bf16[128,2112]{1,0:T(8,128)(2,1)} %bitcast.21, f32[1408]{0:T(1024)} %gain_ref.3, bf16[2112,1408]{1,0:T(8,128)(2,1)} %bitcast.18, f32[1,1408]{1,0:T(1,128)} %get-tuple-element.13.before_ref), custom_call_target="tpu_custom_call" | custom-call | tf_op jit(solution)/shard_map/attend_1/pallas_call | solution.py:279
  90.6 9.6 %psum.7 = f32[1,1408]{1,0:T(1,128)S(1)} all-reduce(f32[1,1408]{1,0:T(1,128)} %get-tuple-element.15), channel_id=1, replica_groups={{0,16,32,48},{64,80,96,112},{128,144,160,176},{192,208,224,240},{1,17,3..., use_global_device_ids=true, to_apply=%region_0.0 | all-reduce | flops 1408 | bytes 11264 | tf_op jit(solution)/shard_map/psum | solution.py:337
  100.2 1.3 collective-permute-start
  101.5 2.5 %collective-permute-start.1 = (f32[1,1408]{1,0:T(1,128)S(1)}, f32[1,1408]{1,0:T(1,128)S(1)}, u32[]{:S(2)}, u32[]{:S(2)}) collective-permute-start(f32[1,1408]{1,0:T(1,128)S(1)} %psum.7), channel_id=1, source_target_pairs={{0,128},{16,144},{32,160},{48,176},{64,192},{80,208},{96,224},{112... | collective-permute-start | bytes 16904 | tf_op jit(solution)/shard_map/ppermute | solution.py:338
  103.9 1.1 collective-permute-start.2
  105.1 0.0 collective-permute-done
  105.1 0.4 collective-permute-done.1
  105.4 1.2 collective-permute-done.2
  106.8 0.7 bitcast_dynamic-update-slice_fusion
  107.5 3.3 %all-to-all-done.1 = bf16[16,24,1408]{2,1,0:T(8,128)(2,1)S(1)} async-done(((bf16[16,24,1408]{2,1,0:T(8,128)(2,1)}), bf16[16,24,1408]{2,1,0:T(8,128)(2,1)S(1)}, u32[]{:S(2)}, u32[]{:S(2)}) %all-to-all-start.1) | async-done | bytes 1081376 | tf_op jit(solution)/shard_map/all_to_all | solution.py:329
  110.8 22.7 %all_to_all.46 = bf16[16,8,1792]{2,1,0:T(8,128)(2,1)S(1)} all-to-all(bf16[16,8,1792]{2,1,0:T(8,128)(2,1)} %bitcast.24), channel_id=1, replica_groups=mesh['dp'=16,'ctx'=16] {'ctx'}, dimensions={0} | all-to-all | bytes 917504 | tf_op jit(solution)/shard_map/all_to_all | solution.py:329
  133.5 0.0 copy-done
  133.5 1.7 %finish.1 = (bf16[2,256,1408]{2,1,0:T(8,128)(2,1)}, f32[1408]{0:T(1024)}) custom-call(bf16[2,256,1408]{2,1,0:T(8,128)(2,1)S(1)} %copy-done, bf16[384,1408]{1,0:T(8,128)(2,1)S(1)} %bitcast.15, bf16[128,1792]{1,0:T(8,128)(2,1)S(1)} %bitcast.16), custom_call_target="tpu_custom_call" | custom-call | tf_op jit(solution)/shard_map/finish/pallas_call | solution.py:303
  (8 shorter events, 0.1 us)
Async XLA Ops:
  5.1 50.4 %all-to-all-start = ((bf16[16,24,2112]{2,1,0:T(8,128)(2,1)}), bf16[16,24,2112]{2,1,0:T(8,128)(2,1)S(1)}, u32[]{:S(2)}, u32[]{:S(2)}) async-start(bf16[16,24,2112]{2,1,0:T(8,128)(2,1)} %bitcast.20), calls=%async_computation | async-start | bytes 3342336 | tf_op jit(solution)/shard_map/all_to_all | solution.py:329
  55.5 4.4 %copy-start.1 = (bf16[16,24,2112]{2,1,0:T(8,128)(2,1)}, bf16[16,24,2112]{2,1,0:T(8,128)(2,1)S(1)}, u32[]{:S(2)}) copy-start(bf16[16,24,2112]{2,1,0:T(8,128)(2,1)S(1)} %all-to-all-done) | copy-start | bytes 4866052
  55.5 22.4 %all-to-all-start.2 = ((bf16[16,8,2112]{2,1,0:T(8,128)(2,1)}), bf16[16,8,2112]{2,1,0:T(8,128)(2,1)S(1)}, u32[]{:S(2)}, u32[]{:S(2)}) async-start(bf16[16,8,2112]{2,1,0:T(8,128)(2,1)} %bitcast.22), calls=%async_computation.2 | async-start | bytes 1114112 | tf_op jit(solution)/shard_map/all_to_all | solution.py:329
  77.9 4.3 %copy-start.2 = (bf16[16,8,2112]{2,1,0:T(8,128)(2,1)}, bf16[16,8,2112]{2,1,0:T(8,128)(2,1)S(1)}, u32[]{:S(2)}) copy-start(bf16[16,8,2112]{2,1,0:T(8,128)(2,1)S(1)} %all-to-all-done.2) | copy-start | bytes 1622020
  77.9 32.9 %all-to-all-start.1 = ((bf16[16,24,1408]{2,1,0:T(8,128)(2,1)}), bf16[16,24,1408]{2,1,0:T(8,128)(2,1)S(1)}, u32[]{:S(2)}, u32[]{:S(2)}) async-start(bf16[16,24,1408]{2,1,0:T(8,128)(2,1)} %bitcast.23), calls=%async_computation.1 | async-start | bytes 2162688 | tf_op jit(solution)/shard_map/all_to_all | solution.py:329
  82.2 51.3 %copy-start = (bf16[2,256,1408]{2,1,0:T(8,128)(2,1)S(1)}, bf16[2,256,1408]{2,1,0:T(8,128)(2,1)}, u32[]{:S(2)}) copy-start(bf16[2,256,1408]{2,1,0:T(8,128)(2,1)} %cot_ref.1) | copy-start | bytes 4325380
  100.2 4.9 %collective-permute-start = (f32[1,1408]{1,0:T(1,128)S(1)}, f32[1,1408]{1,0:T(1,128)S(1)}, u32[]{:S(2)}, u32[]{:S(2)}) collective-permute-start(f32[1,1408]{1,0:T(1,128)S(1)} %psum.7), channel_id=1, source_target_pairs={{0,64},{16,80},{32,96},{48,112},{64,128},{80,144},{96,160},{112,17... | collective-permute-start | bytes 16904 | tf_op jit(solution)/shard_map/ppermute | solution.py:338
  101.5 4.0 %collective-permute-start.1 = (f32[1,1408]{1,0:T(1,128)S(1)}, f32[1,1408]{1,0:T(1,128)S(1)}, u32[]{:S(2)}, u32[]{:S(2)}) collective-permute-start(f32[1,1408]{1,0:T(1,128)S(1)} %psum.7), channel_id=1, source_target_pairs={{0,128},{16,144},{32,160},{48,176},{64,192},{80,208},{96,224},{112... | collective-permute-start | bytes 16904 | tf_op jit(solution)/shard_map/ppermute | solution.py:338
  103.9 2.8 %collective-permute-start.2 = (f32[1,1408]{1,0:T(1,128)S(1)}, f32[1,1408]{1,0:T(1,128)S(1)}, u32[]{:S(2)}, u32[]{:S(2)}) collective-permute-start(f32[1,1408]{1,0:T(1,128)S(1)} %psum.7), channel_id=1, source_target_pairs={{0,192},{16,208},{32,224},{48,240},{64,0},{80,16},{96,32},{112,48}... | collective-permute-start | bytes 16904 | tf_op jit(solution)/shard_map/ppermute | solution.py:338
